TPU v7x, 256 devices: a whole 4x4x8 slice. The times are simulated.
256 devices in a mesh: row: 8 (over z), col: 8 (over y, core), depth: 4 (over x).
Axes of the slice: x: 4, y: 4, z: 8, core: 2. Of those that a mesh axis runs over, the one named last changes fastest.
Arguments:
- features: bfloat16 [512, 6144], P(('col', 'depth'), 'row')
- cotangent: bfloat16 [512, 6144], P(('col', 'depth'), 'row')
- gate_master: float32 [6144, 24576], P('row', ('col', 'depth'))
- up_master: float32 [6144, 24576], P('row', ('col', 'depth'))
- down_master: float32 [24576, 6144], P(('col', 'depth'), 'row')
Outputs:
- gate_gradient: bfloat16 [6144, 24576], P('row', ('col', 'depth'))
- up_gradient: bfloat16 [6144, 24576], P('row', ('col', 'depth'))
- down_gradient: bfloat16 [24576, 6144], P(('col', 'depth'), 'row')
All inputs are finite; a program needn't handle non-finite values.
Results may differ from a plain program's by a relative error of at most 0.0075.
Values may be sent and summed in bfloat16 or wider, within the bound.
A program may use at most 64 MiB of HBM per device.

v0:
```python
import jax
import jax.numpy as jnp
from jax import lax
from jax.sharding import PartitionSpec as P

radius = 0.3


def pointwise(gate_sum, up_sum, back_sum):
    sigmoid_gate = jax.nn.sigmoid(gate_sum)
    swish_gate = gate_sum * sigmoid_gate
    activation = (swish_gate * up_sum).astype(jnp.bfloat16)
    gate_delta = (
        back_sum * up_sum * sigmoid_gate * (1.0 + gate_sum * (1.0 - sigmoid_gate))
    ).astype(jnp.bfloat16)
    up_delta = (back_sum * swish_gate).astype(jnp.bfloat16)
    return (activation, gate_delta, up_delta)


def stacked_terms(token_rows, target_rows, gate_weight, up_weight, down_weight):
    gate_part = jnp.dot(token_rows, gate_weight, preferred_element_type=jnp.float32)
    up_part = jnp.dot(token_rows, up_weight, preferred_element_type=jnp.float32)
    back_part = lax.dot_general(
        target_rows, down_weight, (((1,), (1,)), ((), ())), preferred_element_type=jnp.float32
    )
    return jnp.concatenate([gate_part, up_part, back_part], axis=1)


def pass_gradients(tokens_all, targets_all, gate_weight, up_weight, down_weight):
    hidden_width = gate_weight.shape[1]
    summed = lax.psum_scatter(
        stacked_terms(tokens_all, targets_all, gate_weight, up_weight, down_weight),
        "row",
        scatter_dimension=0,
        tiled=True,
    )
    share_act, share_gate, share_up = pointwise(
        summed[:, :hidden_width],
        summed[:, hidden_width : 2 * hidden_width],
        summed[:, 2 * hidden_width :],
    )
    activation, gate_delta, up_delta = (
        lax.all_gather(share_act, "row", axis=0, tiled=True),
        lax.all_gather(share_gate, "row", axis=0, tiled=True),
        lax.all_gather(share_up, "row", axis=0, tiled=True),
    )
    contract = (((0,), (0,)), ((), ()))
    gate_grad = lax.dot_general(
        tokens_all, gate_delta, contract, preferred_element_type=jnp.float32
    )
    up_grad = lax.dot_general(tokens_all, up_delta, contract, preferred_element_type=jnp.float32)
    down_grad = lax.dot_general(
        activation, targets_all, contract, preferred_element_type=jnp.float32
    )
    return (gate_grad, up_grad, down_grad)


def shards(features, cotangent, gate_master, up_master, down_master):
    tokens_all, targets_all = (
        lax.all_gather(features, ("col", "depth"), axis=0, tiled=True),
        lax.all_gather(cotangent, ("col", "depth"), axis=0, tiled=True),
    )
    weight_local = (
        jnp.sum(gate_master * gate_master)
        + jnp.sum(up_master * up_master)
        + jnp.sum(down_master * down_master)
    )
    first_gate, first_up, first_down = pass_gradients(
        tokens_all,
        targets_all,
        gate_master.astype(jnp.bfloat16),
        up_master.astype(jnp.bfloat16),
        down_master.astype(jnp.bfloat16),
    )
    gradient_local = (
        jnp.sum(first_gate * first_gate)
        + jnp.sum(first_up * first_up)
        + jnp.sum(first_down * first_down)
    )
    weight_energy, gradient_energy = lax.psum(
        (weight_local, gradient_local), ("row", "col", "depth")
    )
    step_scale = radius * jnp.sqrt(weight_energy) / jnp.sqrt(gradient_energy + 1e-06)
    perturbed_gate = (gate_master + step_scale * first_gate).astype(jnp.bfloat16)
    perturbed_up = (up_master + step_scale * first_up).astype(jnp.bfloat16)
    perturbed_down = (down_master + step_scale * first_down).astype(jnp.bfloat16)
    gate_grad, up_grad, down_grad = pass_gradients(
        tokens_all, targets_all, perturbed_gate, perturbed_up, perturbed_down
    )
    return (
        gate_grad.astype(jnp.bfloat16),
        up_grad.astype(jnp.bfloat16),
        down_grad.astype(jnp.bfloat16),
    )


def solution(mesh):
    placed = (
        P(("col", "depth"), "row"),
        P(("col", "depth"), "row"),
        P("row", ("col", "depth")),
        P("row", ("col", "depth")),
        P(("col", "depth"), "row"),
    )
    return jax.shard_map(
        shards,
        mesh=mesh,
        in_specs=placed,
        out_specs=(
            P("row", ("col", "depth")),
            P("row", ("col", "depth")),
            P(("col", "depth"), "row"),
        ),
        check_vma=False,
    )
```

profile of v0, /device:TPU:2, one launch (start us, length us, event | category | flops | bytes accessed | tf_op | source)
XLA Modules:
  0.0 491.1 jit_solution(12173461204058244040)
XLA Ops:
  7.2 43.7 %all_gather.24 = bf16[512,768]{1,0:T(8,128)(2,1)S(1)} all-gather(bf16[16,768]{1,0:T(8,128)(2,1)} %param.5), channel_id=1, replica_groups=mesh['row'=8,'col'=8,'depth'=4] {'col','depth'}, dimensions={0}, use_global_device_ids=true | all-gather | bytes 811008 | tf_op jit(solution)/shard_map/all_gather | solution.py:60
  50.9 42.3 %all_gather.25 = bf16[512,768]{1,0:T(8,128)(2,1)S(1)} all-gather(bf16[16,768]{1,0:T(8,128)(2,1)} %param.6), channel_id=1, replica_groups=mesh['row'=8,'col'=8,'depth'=4] {'col','depth'}, dimensions={0}, use_global_device_ids=true | all-gather | bytes 811008 | tf_op jit(solution)/shard_map/all_gather | solution.py:61
  93.2 2.8 fusion.11
  98.5 2.4 pad_maximum_fusion
  101.0 2.0 copy.8
  103.0 2.9 multiply_reduce_fusion.4
  107.2 2.9 multiply_reduce_fusion.3
  110.8 52.7 %reduce-scatter.3.cloned.1.call-done = f32[64,2304]{1,0:T(8,128)} async-done(((f32[512,2304]{1,0:T(8,128)}), f32[64,2304]{1,0:T(8,128)}) %reduce-scatter.3.cloned.1.call-update) | async-done | bytes 589840 | tf_op jit(solution)/shard_map/reduce_scatter | solution.py:31
  164.7 26.2 %all_gather.27 = bf16[512,768]{1,0:T(8,128)(2,1)S(1)} all-gather(bf16[64,768]{1,0:T(8,128)(2,1)S(1)} %get-tuple-element.11), channel_id=1, replica_groups=mesh['row'=8,'col'=8,'depth'=4] {'row'}, dimensions={0}, use_global_device_ids=true | all-gather | bytes 884736 | tf_op jit(solution)/shard_map/all_gather | solution.py:45
  190.9 26.3 %all_gather.26 = bf16[512,768]{1,0:T(8,128)(2,1)S(1)} all-gather(bf16[64,768]{1,0:T(8,128)(2,1)S(1)} %get-tuple-element.12), channel_id=1, replica_groups=mesh['row'=8,'col'=8,'depth'=4] {'row'}, dimensions={0}, use_global_device_ids=true | all-gather | bytes 884736 | tf_op jit(solution)/shard_map/all_gather | solution.py:44
  217.2 26.0 %all_gather.28 = bf16[512,768]{1,0:T(8,128)(2,1)S(1)} all-gather(bf16[64,768]{1,0:T(8,128)(2,1)S(1)} %get-tuple-element.13), channel_id=1, replica_groups=mesh['row'=8,'col'=8,'depth'=4] {'row'}, dimensions={0}, use_global_device_ids=true | all-gather | bytes 884736 | tf_op jit(solution)/shard_map/all_gather | solution.py:43
  243.2 2.9 multiply_reduce_fusion
  246.1 2.8 multiply_reduce_fusion.2
  248.9 2.8 multiply_reduce_fusion.1
  253.7 2.0 copy.10
  255.6 74.5 %all-reduce = (f32[]{:T(128)}, f32[]{:T(128)}) all-reduce(f32[]{:T(128)S(6)} %add.45, f32[]{:T(128)S(6)} %add.49), channel_id=1, replica_groups=mesh['row'=8,'col'=8,'depth'=4] {'row','col','depth'}, use_global_device_ids=true, to_apply=%region_3.0 | all-reduce | flops 2 | bytes 16 | tf_op jit(solution)/shard_map/psum | solution.py:80
  331.5 3.5 convolution_bitcast_fusion
  338.7 2.4 pad_maximum_fusion.1
  341.2 57.1 %reduce-scatter.5.cloned.1.call-done = f32[64,2304]{1,0:T(8,128)} async-done(((f32[512,2304]{1,0:T(8,128)}), f32[64,2304]{1,0:T(8,128)}) %reduce-scatter.5.cloned.1.call-update) | async-done | bytes 589840 | tf_op jit(solution)/shard_map/reduce_scatter | solution.py:31
  399.5 26.2 %all_gather.31 = bf16[512,768]{1,0:T(8,128)(2,1)S(1)} all-gather(bf16[64,768]{1,0:T(8,128)(2,1)S(1)} %get-tuple-element.8), channel_id=1, replica_groups=mesh['row'=8,'col'=8,'depth'=4] {'row'}, dimensions={0}, use_global_device_ids=true | all-gather | bytes 884736 | tf_op jit(solution)/shard_map/all_gather | solution.py:43
  425.7 1.8 convolution_convert_fusion
  427.5 26.3 %all_gather.29 = bf16[512,768]{1,0:T(8,128)(2,1)S(1)} all-gather(bf16[64,768]{1,0:T(8,128)(2,1)S(1)} %get-tuple-element.9), channel_id=1, replica_groups=mesh['row'=8,'col'=8,'depth'=4] {'row'}, dimensions={0}, use_global_device_ids=true | all-gather | bytes 884736 | tf_op jit(solution)/shard_map/all_gather | solution.py:44
  454.6 1.5 copy.13
  456.1 25.9 %all_gather.30 = bf16[512,768]{1,0:T(8,128)(2,1)S(1)} all-gather(bf16[64,768]{1,0:T(8,128)(2,1)S(1)} %get-tuple-element.10), channel_id=1, replica_groups=mesh['row'=8,'col'=8,'depth'=4] {'row'}, dimensions={0}, use_global_device_ids=true | all-gather | bytes 884736 | tf_op jit(solution)/shard_map/all_gather | solution.py:45
  (33 shorter events, 11.8 us)
Async XLA Ops:
  7.2 156.4 %reduce-scatter.3.cloned.1.call-start = ((), (), s32[]{:S(2)}) async-start(), calls=%async_computation.2 | async-start | bytes 5308416 | tf_op jit(solution)/shard_map/reduce_scatter | solution.py:31
  93.2 3.6 copy-start.5
  93.2 2.8 copy-start
  96.0 1.7 copy-start.2
  101.0 297.3 %reduce-scatter.5.cloned.1.call-start = ((), (), s32[]{:S(2)}) async-start(), calls=%async_computation.3 | async-start | bytes 5308416 | tf_op jit(solution)/shard_map/reduce_scatter | solution.py:31
  110.1 133.1 %copy-start.6 = (bf16[512,768]{1,0:T(8,128)(2,1)S(1)}, bf16[512,768]{1,0:T(8,128)(2,1)}, u32[]{:S(2)}) copy-start(bf16[512,768]{1,0:T(8,128)(2,1)} %copy-done.5) | copy-start | bytes 2359300
  248.9 4.8 copy-start.1
  331.5 3.6 copy-start.3
  331.5 4.0 copy-start.8
  335.5 1.7 copy-start.4
  335.5 2.4 copy-start.9
  341.2 84.5 %copy-start.7 = (bf16[512,768]{1,0:T(8,128)(2,1)S(1)}, bf16[512,768]{1,0:T(8,128)(2,1)}, u32[]{:S(2)}) copy-start(bf16[512,768]{1,0:T(8,128)(2,1)} %copy-done.5) | copy-start | bytes 2359300
Sparse Core Ops, SparseCore 0:
  101.1 62.3 reduce-scatter.2
  341.3 56.9 reduce-scatter.4
where the time goes:
time: 492 us; the launch traced here: 491 us
  blocking collectives  317 us (64%)
  waiting for transfers between devices  110 us (22%)
  matrix products  21.6 us (4%)
  between operations  19.5 us (4%)
  other arithmetic  13.1 us (3%)
  local copies, waits for them, and re-layouts  9.72 us (2%)
    reduce_scatter x2, waiting for transfers between devices, pass_gradients(): lax.psum_scatter(stacked_terms(tokens_all, targets_all, gate_weight, up_w...  110 us
    psum x1, blocking collectives, shards(): lax.psum((weight_local, gradient_local), ('row', 'col', 'depth'))  74.5 us
    all_gather x2, blocking collectives, pass_gradients(): lax.all_gather(share_gate, 'row', axis=0, tiled=True)  52.6 us
    all_gather x2, blocking collectives, pass_gradients(): lax.all_gather(share_act, 'row', axis=0, tiled=True)  52.1 us
    all_gather x2, blocking collectives, pass_gradients(): lax.all_gather(share_up, 'row', axis=0, tiled=True)  52.1 us
    all_gather x1, blocking collectives, shards(): lax.all_gather(features, ('col', 'depth'), axis=0, tiled=True)  43.7 us
    all_gather x1, blocking collectives, shards(): lax.all_gather(cotangent, ('col', 'depth'), axis=0, tiled=True)  42.3 us
  transfers between devices with their start and end apart: 2, of which 2 were waited for; matrix products, arithmetic and copies ran while one was open for 2% of the time, Pallas kernels for 0%

commit v1 on v0

v1 whole, which is shorter than its diff:
```python
import jax
import jax.numpy as jnp
from jax import lax
from jax.sharding import PartitionSpec as P

radius = 0.3
ROW_CONTRACT = (((1,), (1,)), ((), ()))


def pointwise(gate_sum, up_sum, back_sum):
    sigmoid_gate = jax.nn.sigmoid(gate_sum)
    swish_gate = gate_sum * sigmoid_gate
    activation = (swish_gate * up_sum).astype(jnp.bfloat16)
    gate_delta = (
        back_sum * up_sum * sigmoid_gate * (1.0 + gate_sum * (1.0 - sigmoid_gate))
    ).astype(jnp.bfloat16)
    up_delta = (back_sum * swish_gate).astype(jnp.bfloat16)
    return (activation, gate_delta, up_delta)


def split_dot(delta, gram):
    high = gram.astype(jnp.bfloat16)
    low = (gram - high.astype(jnp.float32)).astype(jnp.bfloat16)
    return jnp.dot(delta, high, preferred_element_type=jnp.float32) + jnp.dot(
        delta, low, preferred_element_type=jnp.float32
    )


def shards(features, cotangent, gate_master, up_master, down_master):
    tokens_all, targets_all = (
        lax.all_gather(features, ("col", "depth"), axis=0, tiled=True),
        lax.all_gather(cotangent, ("col", "depth"), axis=0, tiled=True),
    )
    gram_rows = jnp.concatenate(
        [
            lax.dot_general(features, tokens_all, ROW_CONTRACT, preferred_element_type=jnp.float32),
            lax.dot_general(cotangent, targets_all, ROW_CONTRACT, preferred_element_type=jnp.float32),
        ],
        axis=1,
    )
    gram_all = lax.all_gather(
        lax.psum(gram_rows, "row"), ("col", "depth"), axis=0, tiled=True
    )
    tokens_gram, targets_gram = jnp.split(gram_all, 2, axis=1)

    first_contract = (((0,), (1,)), ((), ()))
    gate_weight, up_weight, down_weight = (
        gate_master.astype(jnp.bfloat16),
        up_master.astype(jnp.bfloat16),
        down_master.astype(jnp.bfloat16),
    )
    partial_sums = jnp.stack(
        [
            lax.dot_general(gate_weight, tokens_all, first_contract, preferred_element_type=jnp.float32),
            lax.dot_general(up_weight, tokens_all, first_contract, preferred_element_type=jnp.float32),
            lax.dot_general(down_weight, targets_all, ROW_CONTRACT, preferred_element_type=jnp.float32),
        ]
    )
    sums = lax.psum_scatter(partial_sums, "row", scatter_dimension=1, tiled=True)
    gate_sum, up_sum, back_sum = sums[0], sums[1], sums[2]
    activation, gate_delta, up_delta = pointwise(gate_sum, up_sum, back_sum)
    gate_step = split_dot(gate_delta, tokens_gram)
    up_step = split_dot(up_delta, tokens_gram)
    back_step = split_dot(activation, targets_gram)
    weight_local = (
        jnp.sum(gate_master * gate_master)
        + jnp.sum(up_master * up_master)
        + jnp.sum(down_master * down_master)
    )
    gradient_local = (
        jnp.sum(gate_delta.astype(jnp.float32) * gate_step)
        + jnp.sum(up_delta.astype(jnp.float32) * up_step)
        + jnp.sum(activation.astype(jnp.float32) * back_step)
    )
    weight_energy, gradient_energy = lax.psum(
        (weight_local, gradient_local), ("row", "col", "depth")
    )
    step_scale = radius * jnp.sqrt(weight_energy) / jnp.sqrt(gradient_energy + 1e-06)
    second = jnp.stack(
        pointwise(
            gate_sum + step_scale * gate_step,
            up_sum + step_scale * up_step,
            back_sum + step_scale * back_step,
        )
    )
    second_all = lax.all_gather(second, "row", axis=1, tiled=True)
    last_contract = (((0,), (1,)), ((), ()))
    gate_grad = lax.dot_general(
        tokens_all, second_all[1], last_contract, preferred_element_type=jnp.float32
    )
    up_grad = lax.dot_general(
        tokens_all, second_all[2], last_contract, preferred_element_type=jnp.float32
    )
    down_grad = jnp.dot(second_all[0], targets_all, preferred_element_type=jnp.float32)
    return (
        gate_grad.astype(jnp.bfloat16),
        up_grad.astype(jnp.bfloat16),
        down_grad.astype(jnp.bfloat16),
    )


def solution(mesh):
    placed = (
        P(("col", "depth"), "row"),
        P(("col", "depth"), "row"),
        P("row", ("col", "depth")),
        P("row", ("col", "depth")),
        P(("col", "depth"), "row"),
    )
    return jax.shard_map(
        shards,
        mesh=mesh,
        in_specs=placed,
        out_specs=(
            P("row", ("col", "depth")),
            P("row", ("col", "depth")),
            P(("col", "depth"), "row"),
        ),
        check_vma=False,
    )
```

time: 492 us -> 429 us (0.87)
  blocking collectives: 317 us -> 162 us
  waiting for transfers between devices: 110 us -> 208 us
  local copies, waits for them, and re-layouts: 9.72 us -> 4.76 us
    all_gather x6 -> x0, blocking collectives: 157 us -> none  [the longest x2 52.6 us: pass_gradients(): lax.all_gather(share_gate, 'row', axis=0, tiled=True)]
    all_gather x0 -> x2, waiting for transfers between devices: none -> 87.2 us  [the longest x1 48.1 us: shards(): lax.all_gather(lax.psum(gram_rows, 'row'), ('col', 'depth'), axis=0, tile...]
    psum x0 -> x1, waiting for transfers between devices: none -> 66.6 us  [shards(): lax.psum(gram_rows, 'row')]
    reduce_scatter x2 -> x1, waiting for transfers between devices: 110 us -> 53.7 us  [shards(): lax.psum_scatter(partial_sums, 'row', scatter_dimension=1, tiled=True)]
    unnamed x24 -> x22, local copies, waits for them, and re-layouts: 9.72 us -> 4.76 us
    dot_general x12 -> x14, matrix products: 21.6 us -> 21.4 us  [the longest x3 7.82 us: split_dot(): jnp.dot(delta, low, preferred_element_type=jnp.float32)]
  transfers between devices with their start and end apart: 2 -> 4, of which waited for: 2 -> 4; matrix products, arithmetic and copies ran while one was open for 2% -> 3% of each run, Pallas kernels for 0% -> 0%
where the time goes in v1:
time: 429 us; the launch traced here: 428 us
  waiting for transfers between devices  208 us (48%)
  blocking collectives  162 us (38%)
  matrix products  21.4 us (5%)
  between operations  19 us (4%)
  other arithmetic  12.9 us (3%)
  local copies, waits for them, and re-layouts  4.76 us (1%)
    psum x1, blocking collectives, shards(): lax.psum((weight_local, gradient_local), ('row', 'col', 'depth'))  75.9 us
    psum x1, waiting for transfers between devices, shards(): lax.psum(gram_rows, 'row')  66.6 us
    reduce_scatter x1, waiting for transfers between devices, shards(): lax.psum_scatter(partial_sums, 'row', scatter_dimension=1, tiled=True)  53.7 us
    all_gather x1, waiting for transfers between devices, shards(): lax.all_gather(lax.psum(gram_rows, 'row'), ('col', 'depth'), axis=0, tile...  48.1 us
    all_gather x1, blocking collectives, shards(): lax.all_gather(features, ('col', 'depth'), axis=0, tiled=True)  43.8 us
    all_gather x1, blocking collectives, shards(): lax.all_gather(cotangent, ('col', 'depth'), axis=0, tiled=True)  42.3 us
    all_gather x1, waiting for transfers between devices, shards(): second_all = lax.all_gather(second, 'row', axis=1, tiled=True)  39.1 us
  transfers between devices with their start and end apart: 4, of which 4 were waited for; matrix products, arithmetic and copies ran while one was open for 3% of the time, Pallas kernels for 0%

profile of v1, /device:TPU:2, one launch (start us, length us, event | category | flops | bytes accessed | tf_op | source)
XLA Modules:
  0.0 427.9 jit_solution(3431753894512577312)
XLA Ops:
  7.2 43.8 %all_gather.12 = bf16[512,768]{1,0:T(8,128)(2,1)S(1)} all-gather(bf16[16,768]{1,0:T(8,128)(2,1)} %param.5), channel_id=1, replica_groups=mesh['row'=8,'col'=8,'depth'=4] {'col','depth'}, dimensions={0}, use_global_device_ids=true | all-gather | bytes 811008 | tf_op jit(solution)/shard_map/all_gather | solution.py:31
  51.0 42.3 %all_gather.13 = bf16[512,768]{1,0:T(8,128)(2,1)S(1)} all-gather(bf16[16,768]{1,0:T(8,128)(2,1)} %param.6), channel_id=1, replica_groups=mesh['row'=8,'col'=8,'depth'=4] {'col','depth'}, dimensions={0}, use_global_device_ids=true | all-gather | bytes 811008 | tf_op jit(solution)/shard_map/all_gather | solution.py:32
  93.4 1.0 fusion.13
  95.5 0.8 convolution_bitcast_fusion.1
  99.8 2.6 pad_maximum_fusion
  102.5 66.6 %all-reduce.3.cloned.1.call-done = f32[16,1024]{1,0:T(8,128)} async-done(((f32[16,1024]{1,0:T(8,128)}), f32[16,1024]{1,0:T(8,128)}) %all-reduce.3.cloned.1.call-update) | async-done | bytes 65552 | tf_op jit(solution)/shard_map/psum | solution.py:42
  169.1 2.9 multiply_reduce_fusion.1
  173.3 2.9 multiply_reduce_fusion
  176.9 53.7 %reduce-scatter.2.cloned.1.call-done = f32[3,96,512]{2,1,0:T(8,128)} async-done(((f32[3,768,512]{2,1,0:T(8,128)}), f32[3,96,512]{2,1,0:T(8,128)}) %reduce-scatter.2.cloned.1.call-update) | async-done | bytes 589840 | tf_op jit(solution)/shard_map/reduce_scatter | solution.py:59
  230.6 1.9 multiply_convert_fusion.4
  232.4 48.1 %all-gather.3.cloned.1.call-done = f32[512,1024]{1,0:T(8,128)} async-done(((f32[16,1024]{1,0:T(8,128)}), f32[512,1024]{1,0:T(8,128)}) %all-gather.3.cloned.1.call-update) | async-done | bytes 2097168 | tf_op jit(solution)/shard_map/all_gather | solution.py:41
  280.6 1.6 fusion.12
  282.1 2.8 multiply_reduce_fusion.5
  285.2 2.6 multiply_reduce_fusion.4
  289.1 1.1 fusion.5
  290.2 2.5 multiply_reduce_fusion.3
  293.2 75.9 %all-reduce = (f32[]{:T(128)}, f32[]{:T(128)}) all-reduce(f32[]{:T(128)S(6)} %add.54, f32[]{:T(128)S(6)} %add.61), channel_id=1, replica_groups=mesh['row'=8,'col'=8,'depth'=4] {'row','col','depth'}, use_global_device_ids=true, to_apply=%region_4.0 | all-reduce | flops 2 | bytes 16 | tf_op jit(solution)/shard_map/psum | solution.py:75
  370.5 1.3 fusion.8
  372.5 39.1 %all-gather.5.cloned.1.call-done = bf16[3,768,512]{2,1,0:T(8,128)(2,1)} async-done(((bf16[3,96,512]{2,1,0:T(8,128)(2,1)}), bf16[3,768,512]{2,1,0:T(8,128)(2,1)}) %all-gather.5.cloned.1.call-update) | async-done | bytes 2359312 | tf_op jit(solution)/shard_map/all_gather | solution.py:86
  411.6 1.9 fusion.1
  413.5 1.5 copy.9
  415.0 2.0 fusion
  417.0 1.5 copy.8
  418.4 2.9 convolution_convert_fusion
  (34 shorter events, 5.7 us)
Async XLA Ops:
  7.2 87.3 %copy-start.9 = (bf16[16,768]{1,0:T(8,128)(2,1)S(1)}, bf16[16,768]{1,0:T(8,128)(2,1)}, u32[]{:S(2)}) copy-start(bf16[16,768]{1,0:T(8,128)(2,1)} %param.6) | copy-start | bytes 73732
  7.2 88.3 %copy-start.1 = (f32[768,768]{1,0:T(8,128)S(1)}, f32[768,768]{1,0:T(8,128)}, u32[]{:S(2)}) copy-start(f32[768,768]{1,0:T(8,128)} %param.8) | copy-start | bytes 7077892
  7.2 161.9 %all-reduce.3.cloned.1.call-start = ((), (), s32[]{:S(2)}) async-start(), calls=%async_computation.2 | async-start | bytes 131072 | tf_op jit(solution)/shard_map/psum | solution.py:42
  93.4 1.0 copy-start.4
  95.4 135.2 %reduce-scatter.2.cloned.1.call-start = ((), (), s32[]{:S(2)}) async-start(), calls=%async_computation.1 | async-start | bytes 5308416 | tf_op jit(solution)/shard_map/reduce_scatter | solution.py:59
  95.5 1.7 copy-start.2
  97.1 1.7 copy-start.3
  97.1 1.8 copy-start.5
  102.4 178.1 %all-gather.3.cloned.1.call-start = ((), (), s32[]{:S(2)}) async-start(), calls=%async_computation.3 | async-start | bytes 2162688 | tf_op jit(solution)/shard_map/all_gather | solution.py:41
  169.1 242.5 %all-gather.5.cloned.1.call-start = ((), (), s32[]{:S(2)}) async-start(), calls=%async_computation.4 | async-start | bytes 2654208 | tf_op jit(solution)/shard_map/all_gather | solution.py:86
  232.4 52.5 %copy-start.8 = (bf16[96,512]{1,0:T(8,128)(2,1)}, bf16[96,512]{1,0:T(8,128)(2,1)S(1)}, u32[]{:S(2)}) copy-start(bf16[96,512]{1,0:T(8,128)(2,1)S(1)} %get-tuple-element.11) | copy-start | bytes 294916
  280.5 4.4 %copy-start = (f32[512,1024]{1,0:T(8,128)S(1)}, f32[512,1024]{1,0:T(8,128)}, u32[]{:S(2)}) copy-start(f32[512,1024]{1,0:T(8,128)} %all-gather.3.cloned.1.call-done) | copy-start | bytes 6291460
  285.2 85.3 %copy-start.7 = (f32[3,96,512]{2,1,0:T(8,128)S(1)}, f32[3,96,512]{2,1,0:T(8,128)}, u32[]{:S(2)}) copy-start(f32[3,96,512]{2,1,0:T(8,128)} %reduce-scatter.2.cloned.1.call-done) | copy-start | bytes 1769476
  415.0 3.4 copy-start.6
Sparse Core Ops, SparseCore 0:
  95.5 73.4 all-reduce.2
  171.8 58.7 reduce-scatter.1
  233.5 47.0 all-gather.2
  372.7 38.9 all-gather.4

commit v2 on v0

v2 whole, which is shorter than its diff:
```python
import functools

import jax
import jax.numpy as jnp
from jax import lax
from jax.experimental import pallas as pl
from jax.experimental.pallas import tpu as pltpu
from jax.sharding import PartitionSpec as P

radius = 0.3
MESH = pl.DeviceIdType.MESH
NT = (((1,), (1,)), ((), ()))
f32, bf16 = jnp.float32, jnp.bfloat16


def pointwise(gate_sum, up_sum, back_sum):
    sigmoid_gate = jax.nn.sigmoid(gate_sum)
    swish_gate = gate_sum * sigmoid_gate
    activation = (swish_gate * up_sum).astype(bf16)
    gate_delta = (
        back_sum * up_sum * sigmoid_gate * (1.0 + gate_sum * (1.0 - sigmoid_gate))
    ).astype(bf16)
    up_delta = (back_sum * swish_gate).astype(bf16)
    return (activation, gate_delta, up_delta)


def fold(x):
    rows, lanes = x.shape
    x = jnp.sum(x.reshape(rows // 8, 8, lanes), axis=0)
    return sum(x[:, i : i + 128] for i in range(0, lanes, 128))


def kernel(
    NZ, NY, NX,
    features, cotangent, gate_master, up_master, down_master,
    deltas_out, tokens_t_out, targets_out,
    tok, tgt, stage, weights, tokens_t, part, outbox, inbox,
    kpart, kin, kown, kf, kc, gram, sums, steps, deltas, energy, energy_in,
    local_sem, tok_s, tok_r, k_s, k_r, kz_s, kz_r, ch_s, ch_r, ag_s, ag_r, en_s, en_r,
):
    z, c, x = lax.axis_index("row"), lax.axis_index("col"), lax.axis_index("depth")
    y, k = c // 2, c % 2
    hidden = weights.shape[1]
    tokens = tokens_t.shape[1]
    half = part.shape[3]

    def at_z(i):
        return ((z + i + NZ) % NZ, c, x)

    def at_y(i):
        return (z, ((y + i) % NY) * 2 + k, x)

    def at_x(i):
        return (z, c, (x + i) % NX)

    sibling = (z, y * 2 + (1 - k), x)

    def remote(src, dst, ssem, rsem, device):
        return pltpu.make_async_remote_copy(
            src_ref=src, dst_ref=dst, send_sem=ssem, recv_sem=rsem,
            device_id=device, device_id_type=MESH,
        )

    def arrive(dst, ssem, rsem):
        remote(dst, dst, ssem, rsem, sibling).wait_recv()

    def leave(src, ssem, rsem):
        remote(src, src, ssem, rsem, sibling).wait_send()

    masters = (gate_master, up_master, down_master)
    loads = [pltpu.make_async_copy(masters[m], stage.at[m], local_sem.at[m]) for m in range(3)]
    for load in loads:
        load.start()

    barrier = pltpu.get_barrier_semaphore()
    partners = (
        [at_z(i) for i in range(1, NZ)]
        + [at_y(i) for i in range(1, NY)]
        + [at_x(i) for i in range(1, NX)]
        + [sibling]
    )
    for device in partners:
        pl.semaphore_signal(barrier, inc=1, device_id=device, device_id_type=MESH)
    pl.semaphore_wait(barrier, len(partners))

    def plane_first(a, b, ss, rs):
        for i in range(1, NX):
            remote(a.at[y, k, x], a.at[y, k, x], ss.at[0, 0, i], rs.at[0, 0, i], at_x(i)).start()
        for i in range(1, NY):
            remote(b.at[y, k, x], b.at[y, k, x], ss.at[1, 0, i], rs.at[1, 0, i], at_y(i)).start()

    def plane_second(a, b, ss, rs):
        for i in range(1, NX):
            arrive(a.at[y, k, (x - i + NX) % NX], ss.at[0, 0, i], rs.at[0, 0, i])
        for i in range(1, NY):
            remote(a.at[y, k], a.at[y, k], ss.at[0, 1, i], rs.at[0, 1, i], at_y(i)).start()
        for i in range(1, NY):
            arrive(b.at[(y - i + NY) % NY, k, x], ss.at[1, 0, i], rs.at[1, 0, i])
        for i in range(1, NX):
            remote(b.at[:, k, x], b.at[:, k, x], ss.at[1, 1, i], rs.at[1, 1, i], at_x(i)).start()
        remote(a.at[y, k], a.at[y, k], ss.at[0, 2, 0], rs.at[0, 2, 0], sibling).start()
        remote(b.at[:, k, x], b.at[:, k, x], ss.at[1, 2, 0], rs.at[1, 2, 0], sibling).start()

    def plane_third(a, b, ss, rs):
        for i in range(1, NY):
            part_a = a.at[(y - i + NY) % NY, k]
            arrive(part_a, ss.at[0, 1, i], rs.at[0, 1, i])
            remote(part_a, part_a, ss.at[0, 2, i], rs.at[0, 2, i], sibling).start()
        for i in range(1, NX):
            part_b = b.at[:, k, (x - i + NX) % NX]
            arrive(part_b, ss.at[1, 1, i], rs.at[1, 1, i])
            remote(part_b, part_b, ss.at[1, 2, i], rs.at[1, 2, i], sibling).start()

    def plane_last(a, b, ss, rs):
        for i in range(NY):
            arrive(a.at[(y - i + NY) % NY, 1 - k], ss.at[0, 2, i], rs.at[0, 2, i])
        for i in range(NX):
            arrive(b.at[:, 1 - k, (x - i + NX) % NX], ss.at[1, 2, i], rs.at[1, 2, i])

    def plane_leave(a, b, ss, rs):
        for i in range(1, NX):
            leave(a.at[y, k, x], ss.at[0, 0, i], rs.at[0, 0, i])
        for i in range(1, NY):
            leave(b.at[y, k, x], ss.at[1, 0, i], rs.at[1, 0, i])
        for i in range(1, NY):
            leave(a.at[y, k], ss.at[0, 1, i], rs.at[0, 1, i])
        for i in range(1, NX):
            leave(b.at[:, k, x], ss.at[1, 1, i], rs.at[1, 1, i])
        for i in range(NY):
            leave(a.at[(y - i + NY) % NY, k], ss.at[0, 2, i], rs.at[0, 2, i])
        for i in range(NX):
            leave(b.at[:, k, (x - i + NX) % NX], ss.at[1, 2, i], rs.at[1, 2, i])

    tok[y, k, x] = features[...]
    tgt[y, k, x] = cotangent[...]
    plane_first(tok, tgt, tok_s, tok_r)

    def prepare(m, transpose):
        loads[m].wait()
        rows = 128

        def body(i, total):
            r = pl.ds(pl.multiple_of(i * rows, rows), rows)
            block = stage[m, r, :]
            if transpose:
                weights[m, :, r] = block.astype(bf16).T
            else:
                weights[m, r, :] = block.astype(bf16)
            return total + fold(block * block)

        return lax.fori_loop(0, hidden // rows, body, jnp.zeros((8, 128), f32))

    weight_energy = prepare(0, True)
    plane_second(tok, tgt, tok_s, tok_r)
    weight_energy += prepare(1, True)
    plane_third(tok, tgt, tok_s, tok_r)
    weight_energy += prepare(2, False)
    plane_last(tok, tgt, tok_s, tok_r)

    for own, every, base in ((features, tok, 0), (cotangent, tgt, NZ // 2)):
        rows = lax.dot_general(
            own[...], every[...].reshape(tokens, -1), NT, preferred_element_type=f32
        )
        for j in range(NZ // 2):
            kpart[base + j] = rows[:, j * 128 : (j + 1) * 128]
    for i in range(1, NZ):
        remote(
            kpart.at[(z + i) % NZ], kin.at[i], kz_s.at[0, i], kz_r.at[0, i], at_z(i)
        ).start()

    chains = []
    for d, sign in ((0, 1), (1, -1)):
        for h in range(2):
            chains.append((d, sign, h, NZ // 2 if d == h else NZ // 2 - 1))
    chains.sort(key=lambda chain: -chain[3])

    def chain_send(t, m):
        for d, sign, h, n in chains:
            if t >= n:
                continue
            owner = (z + sign * (n - t) + NZ) % NZ
            total = part[m, owner, h]
            if t > 0:
                arrive(inbox.at[d, t - 1, m, h], ch_s.at[d, t - 1, m, h], ch_r.at[d, t - 1, m, h])
                total = total + inbox[d, t - 1, m, h].astype(f32)
            outbox[d, t, m, h] = total.astype(outbox.dtype)
            remote(
                outbox.at[d, t, m, h], inbox.at[d, t, m, h],
                ch_s.at[d, t, m, h], ch_r.at[d, t, m, h], at_z(sign),
            ).start()

    for m in range(3):
        every = tok if m < 2 else tgt
        wide = hidden // 2
        for i in range(2):
            part[m, i * (NZ // 2) : (i + 1) * (NZ // 2)] = lax.dot_general(
                weights[m, i * wide : (i + 1) * wide, :],
                every[...].reshape(tokens, -1), NT, preferred_element_type=f32,
            ).reshape(NZ // 2, 2, half, tokens)
        chain_send(0, m)

    def loop3(f):
        def body(m, carry):
            f(m)
            return carry

        lax.fori_loop(0, 3, body, 0)

    for i in range(1, NZ):
        arrive(kin.at[i], kz_s.at[0, i], kz_r.at[0, i])
    total = kpart[z]
    for i in range(1, NZ):
        total = total + kin[i]
    kown[z] = total
    for i in range(1, NZ):
        remote(kown.at[z], kown.at[z], kz_s.at[1, i], kz_r.at[1, i], at_z(i)).start()

    loop3(lambda m: chain_send(1, m))

    for i in range(1, NZ):
        arrive(kown.at[(z - i + NZ) % NZ], kz_s.at[1, i], kz_r.at[1, i])
    kf[y, k, x] = kown[0 : NZ // 2]
    kc[y, k, x] = kown[NZ // 2 : NZ]
    plane_first(kf, kc, k_s, k_r)

    tokens_t[...] = tok[...].reshape(tokens, -1).T
    copies = [
        pltpu.make_async_copy(tokens_t, tokens_t_out, local_sem.at[0]),
        pltpu.make_async_copy(tgt, targets_out, local_sem.at[1]),
    ]
    for copy in copies:
        copy.start()

    loop3(lambda m: chain_send(2, m))
    plane_second(kf, kc, k_s, k_r)
    loop3(lambda m: chain_send(3, m))
    plane_third(kf, kc, k_s, k_r)

    plane_last(kf, kc, k_s, k_r)
    for j in range(NZ // 2):
        for g, every in enumerate((kf, kc)):
            block = every[:, :, :, j].reshape(tokens, 128)
            high = block.astype(bf16)
            gram[g, 0, :, j * 128 : (j + 1) * 128] = high
            gram[g, 1, :, j * 128 : (j + 1) * 128] = (block - high.astype(f32)).astype(bf16)

    def chain_last(m):
        for h in range(2):
            total = part[m, z, h]
            for d, sign, h2, n in chains:
                if h2 != h:
                    continue
                arrive(inbox.at[d, n - 1, m, h], ch_s.at[d, n - 1, m, h], ch_r.at[d, n - 1, m, h])
                total = total + inbox[d, n - 1, m, h].astype(f32)
            sums[m, h] = total

    loop3(chain_last)

    own = 2 * half
    gate_sum, up_sum, back_sum = (sums[m].reshape(own, tokens) for m in range(3))
    activation, gate_delta, up_delta = pointwise(gate_sum, up_sum, back_sum)

    def gram_dot(delta, g):
        return jnp.dot(delta, gram[g, 0], preferred_element_type=f32) + jnp.dot(
            delta, gram[g, 1], preferred_element_type=f32
        )

    both = gram_dot(jnp.concatenate([gate_delta, up_delta], axis=0), 0)
    back_step = gram_dot(activation, 1)
    gate_step, up_step = both[:own], both[own:]
    steps[0], steps[1], steps[2] = gate_step, up_step, back_step
    gradient_energy = (
        fold(gate_delta.astype(f32) * gate_step)
        + fold(up_delta.astype(f32) * up_step)
        + fold(activation.astype(f32) * back_step)
    )
    both_energy = jnp.concatenate(
        [
            jnp.sum(weight_energy, axis=0, keepdims=True),
            jnp.sum(gradient_energy, axis=0, keepdims=True),
            jnp.zeros((6, 128), f32),
        ],
        axis=0,
    )
    for axis, (count, where) in enumerate(
        ((NX, at_x), (NY, at_y), (2, lambda i: sibling), (NZ, at_z))
    ):
        energy[axis] = both_energy
        for i in range(1, count):
            remote(
                energy.at[axis], energy_in.at[axis, i], en_s.at[axis, i], en_r.at[axis, i], where(i)
            ).start()
        for i in range(1, count):
            arrive(energy_in.at[axis, i], en_s.at[axis, i], en_r.at[axis, i])
            both_energy = both_energy + energy_in[axis, i]
    totals = jnp.sum(both_energy, axis=1, keepdims=True)
    step_scale = (
        radius * jnp.sqrt(totals[0:1]) / jnp.sqrt(jnp.maximum(totals[1:2], 0.0) + 1e-06)
    )

    second = pointwise(
        sums[0].reshape(own, tokens) + step_scale * steps[0],
        sums[1].reshape(own, tokens) + step_scale * steps[1],
        sums[2].reshape(own, tokens) + step_scale * steps[2],
    )

    def spread(t, m):
        for d, sign, h, n in chains:
            owner = (z - sign * t + NZ) % NZ
            block = deltas.at[m, owner, h]
            if 0 < t <= n:
                arrive(block, ag_s.at[d, t - 1, m, h], ag_r.at[d, t - 1, m, h])
            if t < n:
                remote(
                    block, block, ag_s.at[d, t, m, h], ag_r.at[d, t, m, h], at_z(sign)
                ).start()

    for m in range(3):
        deltas[m, z] = second[m].reshape(2, half, tokens)
        spread(0, m)
    for t in range(1, NZ // 2 + 1):
        loop3(functools.partial(spread, t))
    last = pltpu.make_async_copy(deltas, deltas_out, local_sem.at[2])
    last.start()

    plane_leave(tok, tgt, tok_s, tok_r)
    plane_leave(kf, kc, k_s, k_r)
    for i in range(1, NZ):
        leave(kpart.at[(z + i) % NZ], kz_s.at[0, i], kz_r.at[0, i])
        leave(kown.at[z], kz_s.at[1, i], kz_r.at[1, i])
    for axis, count in enumerate((NX, NY, 2, NZ)):
        for i in range(1, count):
            leave(energy.at[axis], en_s.at[axis, i], en_r.at[axis, i])

    def chains_leave(m):
        for d, sign, h, n in chains:
            for t in range(n):
                leave(outbox.at[d, t, m, h], ch_s.at[d, t, m, h], ch_r.at[d, t, m, h])
                leave(deltas.at[m, (z - sign * t + NZ) % NZ, h], ag_s.at[d, t, m, h], ag_r.at[d, t, m, h])

    loop3(chains_leave)
    for copy in copies:
        copy.wait()
    last.wait()


def shards(NZ, NY, NX, features, cotangent, gate_master, up_master, down_master):
    block, depth = features.shape
    hidden = gate_master.shape[1]
    tokens = block * NY * 2 * NX
    half = hidden // NZ // 2
    hops = NZ // 2
    vmem = pltpu.VMEM
    dma = pltpu.SemaphoreType.DMA
    plane = (NY, 2, NX)
    scratch = [
        vmem(plane + (block, depth), bf16),
        vmem(plane + (block, depth), bf16),
        vmem((3, depth, hidden), f32),
        vmem((3, hidden, depth), bf16),
        vmem((depth, tokens), bf16),
        vmem((3, NZ, 2, half, tokens), f32),
        vmem((2, hops, 3, 2, half, tokens), bf16),
        vmem((2, hops, 3, 2, half, tokens), bf16),
        vmem((NZ, block, 128), f32),
        vmem((NZ, block, 128), f32),
        vmem((NZ, block, 128), f32),
        vmem(plane + (NZ // 2, block, 128), f32),
        vmem(plane + (NZ // 2, block, 128), f32),
        vmem((2, 2, tokens, tokens), bf16),
        vmem((3, 2, half, tokens), f32),
        vmem((3, 2 * half, tokens), f32),
        vmem((3, NZ, 2, half, tokens), bf16),
        vmem((4, 8, 128), f32),
        vmem((4, NZ, 8, 128), f32),
        dma((3,)),
        dma((2, 3, NX)),
        dma((2, 3, NX)),
        dma((2, 3, NX)),
        dma((2, 3, NX)),
        dma((2, NZ)),
        dma((2, NZ)),
        dma((2, hops, 3, 2)),
        dma((2, hops, 3, 2)),
        dma((2, hops, 3, 2)),
        dma((2, hops, 3, 2)),
        dma((4, NZ)),
        dma((4, NZ)),
    ]
    whole = pl.BlockSpec(memory_space=vmem)
    away = pl.BlockSpec(memory_space=pl.ANY)
    deltas, tokens_t, targets = pl.pallas_call(
        functools.partial(kernel, NZ, NY, NX),
        out_shape=(
            jax.ShapeDtypeStruct((3, NZ, 2, half, tokens), bf16),
            jax.ShapeDtypeStruct((depth, tokens), bf16),
            jax.ShapeDtypeStruct(plane + (block, depth), bf16),
        ),
        in_specs=[whole, whole, away, away, away],
        out_specs=(away, away, away),
        scratch_shapes=scratch,
        compiler_params=pltpu.CompilerParams(
            collective_id=0, has_side_effects=True, vmem_limit_bytes=56 * 1024 * 1024
        ),
        cost_estimate=pl.CostEstimate(
            flops=2 * 3 * hidden * depth * tokens,
            bytes_accessed=4 * 3 * hidden * depth,
            transcendentals=0,
        ),
    )(features, cotangent, gate_master, up_master, down_master)
    deltas = deltas.reshape(3, hidden, tokens)
    targets = targets.reshape(tokens, depth)
    gate_grad = lax.dot_general(tokens_t, deltas[1], NT, preferred_element_type=f32)
    up_grad = lax.dot_general(tokens_t, deltas[2], NT, preferred_element_type=f32)
    down_grad = jnp.dot(deltas[0], targets, preferred_element_type=f32)
    return (gate_grad.astype(bf16), up_grad.astype(bf16), down_grad.astype(bf16))


def solution(mesh):
    placed = (
        P(("col", "depth"), "row"),
        P(("col", "depth"), "row"),
        P("row", ("col", "depth")),
        P("row", ("col", "depth")),
        P(("col", "depth"), "row"),
    )
    return jax.shard_map(
        functools.partial(shards, mesh.shape["row"], mesh.shape["col"] // 2, mesh.shape["depth"]),
        mesh=mesh,
        in_specs=placed,
        out_specs=(
            P("row", ("col", "depth")),
            P("row", ("col", "depth")),
            P(("col", "depth"), "row"),
        ),
        check_vma=False,
    )
```

time: 492 us -> 101 us (0.21)
  blocking collectives: 317 us -> 0 us
  waiting for transfers between devices: 110 us -> 0 us
  Pallas kernels: 0 us -> 90.6 us
  between operations: 19.5 us -> 0.67 us
  matrix products: 21.6 us -> 5.45 us
  other arithmetic: 13.1 us -> 0 us
  local copies, waits for them, and re-layouts: 9.72 us -> 1.94 us
    all_gather x8 -> x0, blocking collectives: 243 us -> none  [the longest x2 52.6 us: pass_gradients(): lax.all_gather(share_gate, 'row', axis=0, tiled=True)]
    reduce_scatter x2 -> x0, waiting for transfers between devices: 110 us -> none  [pass_gradients(): lax.psum_scatter(stacked_terms(tokens_all, targets_all, gate_weight, up_w...]
    pallas_call x0 -> x1, Pallas kernels: none -> 90.6 us  [shards(): pl.pallas_call(functools.partial(kernel, NZ, NY, NX), out_shape=(jax.Shap...]
    psum x1 -> x0, blocking collectives: 74.5 us -> none  [shards(): lax.psum((weight_local, gradient_local), ('row', 'col', 'depth'))]
    dot_general x12 -> x3, matrix products: 21.6 us -> 5.45 us  [the longest x1 1.83 us: shards(): lax.dot_general(tokens_t, deltas[2], NT, preferred_element_type=f32)]
    unnamed x24 -> x4, local copies, waits for them, and re-layouts: 9.72 us -> 0.01 us
    reduce_sum x2 -> x0, other arithmetic: 5.76 us -> none  [the longest x1 2.88 us: shards(): jnp.sum(up_master * up_master)]
  transfers between devices with their start and end apart: 2 -> 0, of which waited for: 2 -> 0; matrix products, arithmetic and copies ran while one was open for 2% -> 0% of each run, Pallas kernels for 0% -> 0%
where the time goes in v2:
time: 101 us; the launch traced here: 98.7 us
  Pallas kernels  90.6 us (90%)
  matrix products  5.45 us (5%)
  local copies, waits for them, and re-layouts  1.94 us (2%)
    pallas_call x1, Pallas kernels, shards(): pl.pallas_call(functools.partial(kernel, NZ, NY, NX), out_shape=(jax.Shap...  90.6 us

profile of v2, /device:TPU:2, one launch (start us, length us, event | category | flops | bytes accessed | tf_op | source)
XLA Modules:
  0.0 98.7 jit_solution(10657740016277214848)
XLA Ops:
  0.6 90.6 %shard_map.76 = (bf16[3,8,2,48,512]{4,3,2,1,0:T(8,128)(2,1)}, bf16[768,512]{1,0:T(8,128)(2,1)}, bf16[4,2,4,16,768]{4,3,2,1,0:T(8,128)(2,1)}) custom-call(bf16[16,768]{1,0:T(8,128)(2,1)} %features.1, bf16[16,768]{1,0:T(8,128)(2,1)} %cotangent.1, f32[768,768]{1,0:T(8,128)} %gate_master.1, f32[768,768]{1,0:T(8,128)} %up_master.1, f32[768,768]{1,0:T(8,128)} %down_master.1), custom_call_target="tpu_custom_call" | custom-call | flops 1811939328 | bytes 7077888 | tf_op jit(solution)/shard_map/pallas_call | solution.py:392
  91.3 0.0 copy-start.1
  91.3 1.9 %fusion = (bf16[1,8,2,48,512]{4,3,2,1,0:T(8,128)(2,1)S(1)}, bf16[1,8,2,48,512]{4,3,2,1,0:T(8,128)(2,1)S(1)}, bf16[1,8,2,48,512]{4,3,2,1,0:T(8,128)(2,1)S(1)}) fusion(bf16[3,8,2,48,512]{4,3,2,1,0:T(8,128)(2,1)} %get-tuple-element.7), kind=kLoop, calls=%fused_computation.3 | loop fusion | bytes 4718592 | tf_op jit(solution)/shard_map/slice | solution.py:415
  93.2 0.0 copy-start
  93.2 0.0 copy-done.1
  93.2 1.8 %convolution_convert_fusion = bf16[768,768]{1,0:T(8,128)(2,1)} fusion(bf16[768,512]{1,0:T(8,128)(2,1)S(1)} %bitcast.12, bf16[512,768]{1,0:T(8,128)(2,1)S(1)} %bitcast.13), kind=kOutput, calls=%fused_computation | convolution fusion | flops 604569600 | bytes 2752512 | tf_op jit(solution)/shard_map/dot_general | solution.py:415
  95.0 0.0 copy-done
  95.0 1.8 %convolution_convert_fusion.1 = bf16[768,768]{1,0:T(8,128)(2,1)} fusion(bf16[768,512]{1,0:T(8,128)(2,1)S(1)} %copy-done, bf16[768,512]{1,0:T(8,128)(2,1)S(1)} %bitcast.11), kind=kOutput, calls=%fused_computation.1 | convolution fusion | flops 604569600 | bytes 2752512 | tf_op jit(solution)/shard_map/dot_general | solution.py:414
  96.9 1.8 %convolution_convert_fusion.2 = bf16[768,768]{1,0:T(8,128)(2,1)} fusion(bf16[768,512]{1,0:T(8,128)(2,1)S(1)} %copy-done, bf16[768,512]{1,0:T(8,128)(2,1)S(1)} %bitcast.10), kind=kOutput, calls=%fused_computation.2 | convolution fusion | flops 604569600 | bytes 2752512 | tf_op jit(solution)/shard_map/dot_general | solution.py:413
Async XLA Ops:
  91.3 2.0 %copy-start.1 = (bf16[4,2,4,16,768]{4,3,2,1,0:T(8,128)(2,1)S(1)}, bf16[4,2,4,16,768]{4,3,2,1,0:T(8,128)(2,1)}, u32[]{:S(2)}) copy-start(bf16[4,2,4,16,768]{4,3,2,1,0:T(8,128)(2,1)} %get-tuple-element.8) | copy-start | bytes 2359300
  93.2 1.8 %copy-start = (bf16[768,512]{1,0:T(8,128)(2,1)S(1)}, bf16[768,512]{1,0:T(8,128)(2,1)}, u32[]{:S(2)}) copy-start(bf16[768,512]{1,0:T(8,128)(2,1)} %get-tuple-element.6) | copy-start | bytes 2359300

commit v3 on v2

v3 whole, which is shorter than its diff:
```python
import functools

import jax
import jax.numpy as jnp
from jax import lax
from jax.experimental import pallas as pl
from jax.experimental.pallas import tpu as pltpu
from jax.sharding import PartitionSpec as P

radius = 0.3
MESH = pl.DeviceIdType.MESH
NT = (((1,), (1,)), ((), ()))
f32, bf16 = jnp.float32, jnp.bfloat16


def pointwise(gate_sum, up_sum, back_sum):
    sigmoid_gate = jax.nn.sigmoid(gate_sum)
    swish_gate = gate_sum * sigmoid_gate
    activation = (swish_gate * up_sum).astype(bf16)
    gate_delta = (
        back_sum * up_sum * sigmoid_gate * (1.0 + gate_sum * (1.0 - sigmoid_gate))
    ).astype(bf16)
    up_delta = (back_sum * swish_gate).astype(bf16)
    return (activation, gate_delta, up_delta)


def fold(x):
    rows, lanes = x.shape
    x = jnp.sum(x.reshape(rows // 8, 8, lanes), axis=0)
    return sum(x[:, i : i + 128] for i in range(0, lanes, 128))


def all_gather_plane(NY, NX, y, k, x, at_x, at_y, sibling, remote, arrive, leave):
    every = slice(None)

    def flow_parts(order):
        if order == "xy":
            first, second = at_x, at_y
            own, line = (y, k, x), (y, k, every)
            one = lambda i: (y, k, (x - i + NX) % NX)
            lines = lambda i, core: ((y - i + NY) % NY, core, every)
            return NX, NY, first, second, own, line, one, lines
        own, line = (y, k, x), (every, k, x)
        one = lambda i: ((y - i + NY) % NY, k, x)
        lines = lambda i, core: (every, core, (x - i + NX) % NX)
        return NY, NX, at_y, at_x, own, line, one, lines

    def start(flow):
        view, order, ss, rs = flow
        n1, n2, first, second, own, line, one, lines = flow_parts(order)
        for i in range(1, n1):
            remote(view(own), view(own), ss.at[0, i], rs.at[0, i], first(i)).start()

    def middle(flow):
        view, order, ss, rs = flow
        n1, n2, first, second, own, line, one, lines = flow_parts(order)
        for i in range(1, n1):
            arrive(view(one(i)), ss.at[0, i], rs.at[0, i])
        for i in range(1, n2):
            remote(view(line), view(line), ss.at[1, i], rs.at[1, i], second(i)).start()
        remote(view(line), view(line), ss.at[2, 0], rs.at[2, 0], sibling).start()

    def across(flow):
        view, order, ss, rs = flow
        n1, n2, first, second, own, line, one, lines = flow_parts(order)
        for i in range(1, n2):
            there = view(lines(i, k))
            arrive(there, ss.at[1, i], rs.at[1, i])
            remote(there, there, ss.at[2, i], rs.at[2, i], sibling).start()

    def finish(flow):
        view, order, ss, rs = flow
        n1, n2, first, second, own, line, one, lines = flow_parts(order)
        for i in range(n2):
            arrive(view(lines(i, 1 - k)), ss.at[2, i], rs.at[2, i])

    def sent(flow):
        view, order, ss, rs = flow
        n1, n2, first, second, own, line, one, lines = flow_parts(order)
        for i in range(1, n1):
            leave(view(own), ss.at[0, i], rs.at[0, i])
        for i in range(1, n2):
            leave(view(line), ss.at[1, i], rs.at[1, i])
        for i in range(n2):
            leave(view(lines(i, k)), ss.at[2, i], rs.at[2, i])

    return start, middle, across, finish, sent


def powers(largest):
    scale = jnp.ones_like(largest)
    inverse = jnp.ones_like(largest)
    for e in (64, 32, 16, 8):
        over = largest >= 2.0**e
        under = largest < 2.0**-e
        down = jnp.where(over, 2.0**-e, jnp.where(under, 2.0**e, 1.0))
        up = jnp.where(over, 2.0**e, jnp.where(under, 2.0**-e, 1.0))
        largest, scale, inverse = largest * down, scale * down, inverse * up
    return scale, inverse


def kernel(
    NZ, NY, NX,
    features, cotangent, gate_master, up_master, down_master,
    deltas_out, tokens_t_out, targets_out,
    tok, tgt, stage, weights, tokens_t, part, outbox, inbox,
    peak, peak_in, kpart, kin, kown, kplane, gram, sums, steps, deltas, energy, energy_in,
    local_sem, out_sem, plane_s, plane_r, peak_s, peak_r, kz_s, kz_r, ch_s, ch_r, ag_s, ag_r, en_s, en_r,
):
    z, c, x = lax.axis_index("row"), lax.axis_index("col"), lax.axis_index("depth")
    y, k = c // 2, c % 2
    hidden = weights.shape[1]
    depth, tokens = tokens_t.shape
    half = part.shape[3]
    block = features.shape[0]
    span = tokens // 128

    def at_z(i):
        return ((z + i + NZ) % NZ, c, x)

    def at_y(i):
        return (z, ((y + i) % NY) * 2 + k, x)

    def at_x(i):
        return (z, c, (x + i) % NX)

    def at_plane(q):
        return (z, ((y + q // NX) % NY) * 2 + k, (x + q % NX) % NX)

    def at_pair(q):
        return ((z + q // 2) % NZ, y * 2 + (k + q % 2) % 2, x)

    sibling = at_pair(1)

    def remote(src, dst, ssem, rsem, device):
        return pltpu.make_async_remote_copy(
            src_ref=src, dst_ref=dst, send_sem=ssem, recv_sem=rsem,
            device_id=device, device_id_type=MESH,
        )

    def arrive(dst, ssem, rsem):
        remote(dst, dst, ssem, rsem, sibling).wait_recv()

    def leave(src, ssem, rsem):
        remote(src, src, ssem, rsem, sibling).wait_send()

    masters = (gate_master, up_master, down_master)
    loads = [pltpu.make_async_copy(masters[m], stage.at[m], local_sem.at[m]) for m in range(3)]
    for load in loads:
        load.start()

    barrier = pltpu.get_barrier_semaphore()
    partners = [at_plane(q) for q in range(1, NY * NX)] + [at_pair(q) for q in range(1, 2 * NZ)]
    for device in partners:
        pl.semaphore_signal(barrier, inc=1, device_id=device, device_id_type=MESH)
    tok[y, k, x] = features[...]
    tgt[y, k, x] = cotangent[...]
    pl.semaphore_wait(barrier, len(partners))

    start, middle, across, finish, sent = all_gather_plane(
        NY, NX, y, k, x, at_x, at_y, sibling, remote, arrive, leave
    )

    def lanes(ref, low, high):
        return lambda where: ref.at[(*where, slice(None), pl.ds(low, high - low))]

    cut = depth // 2
    flows_tok = (
        (lanes(tok, 0, cut), "xy", plane_s.at[0], plane_r.at[0]),
        (lanes(tok, cut, depth), "yx", plane_s.at[1], plane_r.at[1]),
    )
    flows_tgt = (
        (lanes(tgt, 0, cut), "xy", plane_s.at[2], plane_r.at[2]),
        (lanes(tgt, cut, depth), "yx", plane_s.at[3], plane_r.at[3]),
    )
    flows_gram = tuple(
        (lambda where, g=g: kplane.at[(g, *where)], order, plane_s.at[4 + g], plane_r.at[4 + g])
        for g, order in enumerate(("xy", "yx"))
    )

    def run(step, flows):
        for flow in flows:
            step(flow)

    def prepare(m, transpose):
        loads[m].wait()
        rows = 128

        def body(i, total):
            r = pl.ds(pl.multiple_of(i * rows, rows), rows)
            piece = stage[m, r, :]
            if transpose:
                weights[m, :, r] = piece.astype(bf16).T
            else:
                weights[m, r, :] = piece.astype(bf16)
            return total + fold(piece * piece)

        return lax.fori_loop(0, hidden // rows, body, jnp.zeros((8, 128), f32))

    chains = []
    for d, sign in ((0, 1), (1, -1)):
        for h in range(2):
            chains.append((d, sign, h, NZ // 2 if d == h else NZ // 2 - 1))
    chains.sort(key=lambda chain: -chain[3])

    def chain_send(t, m):
        for d, sign, h, n in chains:
            if t >= n:
                continue
            owner = (z + sign * (n - t) + NZ) % NZ
            total = part[m, owner, h]
            if t > 0:
                arrive(inbox.at[d, t - 1, m, h], ch_s.at[d, t - 1, m, h], ch_r.at[d, t - 1, m, h])
                total = total + inbox[d, t - 1, m, h].astype(f32)
            outbox[d, t, m, h] = total.astype(outbox.dtype)
            remote(
                outbox.at[d, t, m, h], inbox.at[d, t, m, h],
                ch_s.at[d, t, m, h], ch_r.at[d, t, m, h], at_z(sign),
            ).start()

    def multiply(m):
        every = tok if m < 2 else tgt
        wide = hidden // 2
        for i in range(2):
            part[m, i * (NZ // 2) : (i + 1) * (NZ // 2)] = lax.dot_general(
                weights[m, i * wide : (i + 1) * wide, :],
                every[...].reshape(tokens, depth), NT, preferred_element_type=f32,
            ).reshape(NZ // 2, 2, half, tokens)

    def loop3(f):
        def body(m, carry):
            f(m)
            return carry

        lax.fori_loop(0, 3, body, 0)

    def peak_send(g, every):
        largest = jnp.max(jnp.abs(every[...].reshape(tokens // 16, 16, depth)), axis=0).astype(f32)
        largest = jnp.max(largest.reshape(2, 8, depth), axis=0)
        largest = functools.reduce(
            jnp.maximum, [largest[:, i : i + 128] for i in range(0, depth, 128)]
        )
        peak[g] = largest
        for i in range(1, NZ):
            remote(peak.at[g], peak_in.at[g, i], peak_s.at[g, i], peak_r.at[g, i], at_z(i)).start()

    def gram_partial(g, own, every):
        largest = peak[g]
        for i in range(1, NZ):
            arrive(peak_in.at[g, i], peak_s.at[g, i], peak_r.at[g, i])
            largest = jnp.maximum(largest, peak_in[g, i])
        largest = jnp.max(jnp.max(largest, axis=0, keepdims=True), axis=1, keepdims=True)
        scale, inverse = powers(largest)
        scaled = (own[...].astype(f32) * scale).astype(bf16)
        rows = lax.dot_general(
            scaled, every[...].reshape(tokens, depth), NT, preferred_element_type=f32
        ) * scale
        for r in range(block // 8):
            for j in range(span):
                kpart[g, r * span + j] = rows[r * 8 : r * 8 + 8, j * 128 : j * 128 + 128]
        for i in range(1, NZ):
            remote(
                kpart.at[g, (z + i) % NZ], kin.at[g, i], kz_s.at[g, 0, i], kz_r.at[g, 0, i], at_z(i)
            ).start()
        return inverse

    def gram_reduce(g):
        total = kpart[g, z]
        for i in range(1, NZ):
            arrive(kin.at[g, i], kz_s.at[g, 0, i], kz_r.at[g, 0, i])
            total = total + kin[g, i]
        kown[g, z] = total
        for i in range(1, NZ):
            remote(
                kown.at[g, z], kown.at[g, z], kz_s.at[g, 1, i], kz_r.at[g, 1, i], at_z(i)
            ).start()

    def gram_rows(g):
        for i in range(1, NZ):
            arrive(kown.at[g, (z - i + NZ) % NZ], kz_s.at[g, 1, i], kz_r.at[g, 1, i])
        first = ((y * 2 + k) * NX + x) * block
        rows = lax.broadcasted_iota(jnp.int32, (block, 128), 0)
        columns = lax.broadcasted_iota(jnp.int32, (block, 128), 1)
        rest = []
        for j in range(span):
            piece = jnp.concatenate([kown[g, r * span + j] for r in range(block // 8)], axis=0)
            high = piece.astype(bf16)
            kplane[g, y, k, x, j] = high
            low = jnp.where(columns + j * 128 == rows + first, piece - high.astype(f32), 0.0)
            rest.append(jnp.sum(low, axis=0, keepdims=True))
        rest.append(jnp.zeros((block - span, 128), f32))
        kplane[g, y, k, x, span] = jnp.concatenate(rest, axis=0).astype(bf16)

    run(start, flows_tok)
    run(start, flows_tgt)
    weight_energy = prepare(0, True)
    run(middle, flows_tok)
    weight_energy += prepare(1, True)
    run(across, flows_tok)
    run(middle, flows_tgt)
    run(finish, flows_tok)
    peak_send(0, tok)
    multiply(0)
    chain_send(0, 0)
    run(across, flows_tgt)
    multiply(1)
    chain_send(0, 1)
    weight_energy += prepare(2, False)
    inverse_tok = gram_partial(0, features, tok)
    run(finish, flows_tgt)
    peak_send(1, tgt)
    multiply(2)
    chain_send(0, 2)
    chain_send(1, 0)
    gram_reduce(0)
    inverse_tgt = gram_partial(1, cotangent, tgt)
    chain_send(1, 1)
    gram_rows(0)
    start(flows_gram[0])
    gram_reduce(1)
    chain_send(1, 2)
    chain_send(2, 0)
    gram_rows(1)
    start(flows_gram[1])

    tokens_t[...] = tok[...].reshape(tokens, depth).T
    copies = [
        pltpu.make_async_copy(tokens_t, tokens_t_out, local_sem.at[0]),
        pltpu.make_async_copy(tgt, targets_out, local_sem.at[1]),
    ]
    for copy in copies:
        copy.start()

    middle(flows_gram[0])
    chain_send(2, 1)
    middle(flows_gram[1])
    chain_send(2, 2)
    across(flows_gram[0])
    chain_send(3, 0)
    across(flows_gram[1])
    chain_send(3, 1)
    chain_send(3, 2)

    rest = []
    for g in range(2):
        finish(flows_gram[g])
        for j in range(span):
            gram[g, :, j * 128 : (j + 1) * 128] = kplane[g, :, :, :, j].reshape(tokens, 128)
        low = kplane[g, :, :, :, span].reshape(tokens // block, block, 128)
        low = jnp.sum(low.astype(f32), axis=0)
        rest.append(jnp.concatenate([low[j : j + 1] for j in range(span)], axis=1))

    def chain_last(m):
        for h in range(2):
            total = part[m, z, h]
            for d, sign, h2, n in chains:
                if h2 != h:
                    continue
                arrive(inbox.at[d, n - 1, m, h], ch_s.at[d, n - 1, m, h], ch_r.at[d, n - 1, m, h])
                total = total + inbox[d, n - 1, m, h].astype(f32)
            sums[m, h] = total

    loop3(chain_last)

    own = 2 * half
    gate_sum, up_sum, back_sum = (sums[m].reshape(own, tokens) for m in range(3))
    activation, gate_delta, up_delta = pointwise(gate_sum, up_sum, back_sum)

    def gram_dot(delta, g, inverse):
        product = jnp.dot(delta, gram[g], preferred_element_type=f32)
        return (product + delta.astype(f32) * rest[g]) * inverse

    both = gram_dot(jnp.concatenate([gate_delta, up_delta], axis=0), 0, inverse_tok)
    back_step = gram_dot(activation, 1, inverse_tgt)
    gate_step, up_step = both[:own], both[own:]
    steps[0], steps[1], steps[2] = gate_step, up_step, back_step
    gradient_energy = (
        fold(gate_delta.astype(f32) * inverse_tok * gate_step)
        + fold(up_delta.astype(f32) * inverse_tok * up_step)
        + fold(activation.astype(f32) * inverse_tgt * back_step)
    )
    both_energy = jnp.concatenate(
        [
            jnp.sum(weight_energy, axis=0, keepdims=True),
            jnp.sum(gradient_energy, axis=0, keepdims=True),
            jnp.zeros((6, 128), f32),
        ],
        axis=0,
    )
    spans = ((NY * NX, at_plane), (2 * NZ, at_pair))
    for axis, (count, where) in enumerate(spans):
        energy[axis] = both_energy
        for q in range(1, count):
            remote(
                energy.at[axis], energy_in.at[axis, q], en_s.at[axis, q], en_r.at[axis, q], where(q)
            ).start()
        for q in range(1, count):
            arrive(energy_in.at[axis, q], en_s.at[axis, q], en_r.at[axis, q])
            both_energy = both_energy + energy_in[axis, q]
    totals = jnp.sum(both_energy, axis=1, keepdims=True)
    step_scale = (
        radius * jnp.sqrt(totals[0:1]) / jnp.sqrt(jnp.maximum(totals[1:2], 0.0) + 1e-06)
    )
    step_tok, step_tgt = step_scale * inverse_tok, step_scale * inverse_tgt

    second = pointwise(
        sums[0].reshape(own, tokens) + step_tok * steps[0],
        sums[1].reshape(own, tokens) + step_tok * steps[1],
        sums[2].reshape(own, tokens) + step_tgt * steps[2],
    )

    def to_hbm(m, owner, h):
        return pltpu.make_async_copy(
            deltas.at[m, owner, h], deltas_out.at[m, owner, h], out_sem.at[m, owner, h]
        )

    def spread(t, m):
        for d, sign, h, n in chains:
            owner = (z - sign * t + NZ) % NZ
            there = deltas.at[m, owner, h]
            if 0 < t <= n:
                arrive(there, ag_s.at[d, t - 1, m, h], ag_r.at[d, t - 1, m, h])
            if t < n:
                remote(
                    there, there, ag_s.at[d, t, m, h], ag_r.at[d, t, m, h], at_z(sign)
                ).start()
            if 0 < t <= n:
                to_hbm(m, owner, h).start()

    for m in range(3):
        deltas[m, z] = second[m].reshape(2, half, tokens)
        spread(0, m)

    def own_to_hbm(m):
        for h in range(2):
            to_hbm(m, z, h).start()

    loop3(own_to_hbm)

    for flow in flows_tok + flows_tgt + flows_gram:
        sent(flow)
    for g in range(2):
        for i in range(1, NZ):
            leave(peak.at[g], peak_s.at[g, i], peak_r.at[g, i])
            leave(kpart.at[g, (z + i) % NZ], kz_s.at[g, 0, i], kz_r.at[g, 0, i])
            leave(kown.at[g, z], kz_s.at[g, 1, i], kz_r.at[g, 1, i])
    for axis, (count, where) in enumerate(spans):
        for q in range(1, count):
            leave(energy.at[axis], en_s.at[axis, q], en_r.at[axis, q])

    def chains_sent(m):
        for d, sign, h, n in chains:
            for t in range(n):
                leave(outbox.at[d, t, m, h], ch_s.at[d, t, m, h], ch_r.at[d, t, m, h])

    loop3(chains_sent)
    for copy in copies:
        copy.wait()

    for t in range(1, NZ // 2 + 1):
        loop3(functools.partial(spread, t))

    def spread_sent(m):
        for d, sign, h, n in chains:
            for t in range(n):
                leave(
                    deltas.at[m, (z - sign * t + NZ) % NZ, h],
                    ag_s.at[d, t, m, h], ag_r.at[d, t, m, h],
                )
        for owner in range(NZ):
            for h in range(2):
                to_hbm(m, owner, h).wait()

    loop3(spread_sent)


def gradients(tokens_t, deltas, targets, gate_out, up_out, down_out):
    gate_out[...] = lax.dot_general(
        tokens_t[...], deltas[1], NT, preferred_element_type=f32
    ).astype(bf16)
    up_out[...] = lax.dot_general(
        tokens_t[...], deltas[2], NT, preferred_element_type=f32
    ).astype(bf16)
    down_out[...] = jnp.dot(deltas[0], targets[...], preferred_element_type=f32).astype(bf16)


def shards(NZ, NY, NX, features, cotangent, gate_master, up_master, down_master):
    block, depth = features.shape
    hidden = gate_master.shape[1]
    tokens = block * NY * 2 * NX
    half = hidden // NZ // 2
    hops = NZ // 2
    span = tokens // 128
    vmem = pltpu.VMEM
    dma = pltpu.SemaphoreType.DMA
    plane = (NY, 2, NX)
    scratch = [
        vmem(plane + (block, depth), bf16),
        vmem(plane + (block, depth), bf16),
        vmem((3, depth, hidden), f32),
        vmem((3, hidden, depth), bf16),
        vmem((depth, tokens), bf16),
        vmem((3, NZ, 2, half, tokens), f32),
        vmem((2, hops, 3, 2, half, tokens), bf16),
        vmem((2, hops, 3, 2, half, tokens), bf16),
        vmem((2, 8, 128), f32),
        vmem((2, NZ, 8, 128), f32),
        vmem((2, NZ, 8, 128), f32),
        vmem((2, NZ, 8, 128), f32),
        vmem((2, NZ, 8, 128), f32),
        vmem((2,) + plane + (span + 1, block, 128), bf16),
        vmem((2, tokens, tokens), bf16),
        vmem((3, 2, half, tokens), f32),
        vmem((3, 2 * half, tokens), f32),
        vmem((3, NZ, 2, half, tokens), bf16),
        vmem((2, 8, 128), f32),
        vmem((2, NY * NX, 8, 128), f32),
        dma((3,)),
        dma((3, NZ, 2)),
        dma((6, 3, NX)),
        dma((6, 3, NX)),
        dma((2, NZ)),
        dma((2, NZ)),
        dma((2, 2, NZ)),
        dma((2, 2, NZ)),
        dma((2, hops, 3, 2)),
        dma((2, hops, 3, 2)),
        dma((2, hops, 3, 2)),
        dma((2, hops, 3, 2)),
        dma((2, NY * NX)),
        dma((2, NY * NX)),
    ]
    whole = pl.BlockSpec(memory_space=vmem)
    away = pl.BlockSpec(memory_space=pl.ANY)
    deltas, tokens_t, targets = pl.pallas_call(
        functools.partial(kernel, NZ, NY, NX),
        out_shape=(
            jax.ShapeDtypeStruct((3, NZ, 2, half, tokens), bf16),
            jax.ShapeDtypeStruct((depth, tokens), bf16),
            jax.ShapeDtypeStruct(plane + (block, depth), bf16),
        ),
        in_specs=[whole, whole, away, away, away],
        out_specs=(away, away, away),
        scratch_shapes=scratch,
        compiler_params=pltpu.CompilerParams(
            collective_id=0, has_side_effects=True, vmem_limit_bytes=56 * 1024 * 1024
        ),
        cost_estimate=pl.CostEstimate(
            flops=2 * 3 * hidden * depth * tokens,
            bytes_accessed=4 * 3 * hidden * depth,
            transcendentals=0,
        ),
    )(features, cotangent, gate_master, up_master, down_master)
    tile = hidden // 3
    return pl.pallas_call(
        gradients,
        grid=(hidden // tile,),
        out_shape=(
            jax.ShapeDtypeStruct((depth, hidden), bf16),
            jax.ShapeDtypeStruct((depth, hidden), bf16),
            jax.ShapeDtypeStruct((hidden, depth), bf16),
        ),
        in_specs=[
            pl.BlockSpec((depth, tokens), lambda i: (0, 0)),
            pl.BlockSpec((3, tile, tokens), lambda i: (0, i, 0)),
            pl.BlockSpec((tokens, depth), lambda i: (0, 0)),
        ],
        out_specs=(
            pl.BlockSpec((depth, tile), lambda i: (0, i)),
            pl.BlockSpec((depth, tile), lambda i: (0, i)),
            pl.BlockSpec((tile, depth), lambda i: (i, 0)),
        ),
        compiler_params=pltpu.CompilerParams(vmem_limit_bytes=48 * 1024 * 1024),
        cost_estimate=pl.CostEstimate(
            flops=2 * 3 * hidden * depth * tokens,
            bytes_accessed=2 * (5 * hidden * tokens + 3 * hidden * depth),
            transcendentals=0,
        ),
    )(tokens_t, deltas.reshape(3, hidden, tokens), targets.reshape(tokens, depth))


def solution(mesh):
    placed = (
        P(("col", "depth"), "row"),
        P(("col", "depth"), "row"),
        P("row", ("col", "depth")),
        P("row", ("col", "depth")),
        P(("col", "depth"), "row"),
    )
    return jax.shard_map(
        functools.partial(shards, mesh.shape["row"], mesh.shape["col"] // 2, mesh.shape["depth"]),
        mesh=mesh,
        in_specs=placed,
        out_specs=(
            P("row", ("col", "depth")),
            P("row", ("col", "depth")),
            P(("col", "depth"), "row"),
        ),
        check_vma=False,
    )
```

time: 101 us -> 104 us (1.030)
  Pallas kernels: 90.6 us -> 97.3 us
  matrix products: 5.45 us -> 0 us
  local copies, waits for them, and re-layouts: 1.94 us -> 3.92 us
    dot_general x3 -> x0, matrix products: 5.45 us -> none  [the longest x1 1.83 us: shards(): lax.dot_general(tokens_t, deltas[2], NT, preferred_element_type=f32)]
    unnamed x4 -> x6, local copies, waits for them, and re-layouts: 0.01 us -> 3.92 us
    pallas_call x0 -> x1, Pallas kernels: none -> 3.49 us  [shards(): pl.pallas_call(gradients, grid=(hidden // tile,), out_shape=(jax.ShapeDty...]
    pallas_call x1, Pallas kernels: 90.6 us -> 93.8 us  [shards(): pl.pallas_call(functools.partial(kernel, NZ, NY, NX), out_shape=(jax.Shap...]
    slice x1 -> x0, local copies, waits for them, and re-layouts: 1.93 us -> none  [shards(): down_grad = jnp.dot(deltas[0], targets, preferred_element_type=f32)]
where the time goes in v3:
time: 104 us; the launch traced here: 102 us
  Pallas kernels  97.3 us (94%)
  local copies, waits for them, and re-layouts  3.92 us (4%)
    pallas_call x1, Pallas kernels, shards(): pl.pallas_call(functools.partial(kernel, NZ, NY, NX), out_shape=(jax.Shap...  93.8 us
    unnamed x6, local copies, waits for them, and re-layouts  3.92 us
    pallas_call x1, Pallas kernels, shards(): pl.pallas_call(gradients, grid=(hidden // tile,), out_shape=(jax.ShapeDty...  3.49 us

profile of v3, /device:TPU:2, one launch (start us, length us, event | category | flops | bytes accessed | tf_op | source)
XLA Modules:
  0.0 101.9 jit_solution(4209771090579384588)
XLA Ops:
  0.6 93.8 %shard_map.76 = (bf16[3,8,2,48,512]{4,3,2,1,0:T(8,128)(2,1)}, bf16[768,512]{1,0:T(8,128)(2,1)}, bf16[4,2,4,16,768]{4,3,2,1,0:T(8,128)(2,1)}) custom-call(bf16[16,768]{1,0:T(8,128)(2,1)} %features.1, bf16[16,768]{1,0:T(8,128)(2,1)} %cotangent.1, f32[768,768]{1,0:T(8,128)} %gate_master.1, f32[768,768]{1,0:T(8,128)} %up_master.1, f32[768,768]{1,0:T(8,128)} %down_master.1), custom_call_target="tpu_custom_call" | custom-call | flops 1811939328 | bytes 7077888 | tf_op jit(solution)/shard_map/pallas_call | solution.py:535
  94.5 0.0 copy-start
  94.5 1.7 %copy-done = bf16[3,8,2,48,512]{4,3,2,1,0:T(8,128)(2,1)S(1)} copy-done((bf16[3,8,2,48,512]{4,3,2,1,0:T(8,128)(2,1)S(1)}, bf16[3,8,2,48,512]{4,3,2,1,0:T(8,128)(2,1)}, u32[]{:S(2)}) %copy-start) | copy-done | bytes 2359320
  96.1 0.0 copy-start.1
  96.1 1.1 %copy-done.1 = bf16[768,512]{1,0:T(8,128)(2,1)S(1)} copy-done((bf16[768,512]{1,0:T(8,128)(2,1)S(1)}, bf16[768,512]{1,0:T(8,128)(2,1)}, u32[]{:S(2)}) %copy-start.1) | copy-done | bytes 786456
  97.3 0.0 copy-start.2
  97.3 1.1 %copy-done.2 = bf16[4,2,4,16,768]{4,3,2,1,0:T(8,128)(2,1)S(1)} copy-done((bf16[4,2,4,16,768]{4,3,2,1,0:T(8,128)(2,1)S(1)}, bf16[4,2,4,16,768]{4,3,2,1,0:T(8,128)(2,1)}, u32[]{:S(2)}) %copy-start.2) | copy-done | bytes 786456
  98.4 3.5 %shard_map.77 = (bf16[768,768]{1,0:T(8,128)(2,1)}, bf16[768,768]{1,0:T(8,128)(2,1)}, bf16[768,768]{1,0:T(8,128)(2,1)}) custom-call(bf16[768,512]{1,0:T(8,128)(2,1)S(1)} %copy-done.1, bf16[3,768,512]{2,1,0:T(8,128)(2,1)S(1)} %bitcast.2, bf16[512,768]{1,0:T(8,128)(2,1)S(1)} %bitcast.3), custom_call_target="tpu_custom_call" | custom-call | flops 1811939328 | bytes 7471104 | tf_op jit(solution)/shard_map/pallas_call | solution.py:555
Async XLA Ops:
  94.5 1.7 %copy-start = (bf16[3,8,2,48,512]{4,3,2,1,0:T(8,128)(2,1)S(1)}, bf16[3,8,2,48,512]{4,3,2,1,0:T(8,128)(2,1)}, u32[]{:S(2)}) copy-start(bf16[3,8,2,48,512]{4,3,2,1,0:T(8,128)(2,1)} %get-tuple-element.7) | copy-start | bytes 7077892
  96.1 1.1 %copy-start.1 = (bf16[768,512]{1,0:T(8,128)(2,1)S(1)}, bf16[768,512]{1,0:T(8,128)(2,1)}, u32[]{:S(2)}) copy-start(bf16[768,512]{1,0:T(8,128)(2,1)} %get-tuple-element.6.tokens_t) | copy-start | bytes 2359300
  97.3 1.1 %copy-start.2 = (bf16[4,2,4,16,768]{4,3,2,1,0:T(8,128)(2,1)S(1)}, bf16[4,2,4,16,768]{4,3,2,1,0:T(8,128)(2,1)}, u32[]{:S(2)}) copy-start(bf16[4,2,4,16,768]{4,3,2,1,0:T(8,128)(2,1)} %get-tuple-element.8) | copy-start | bytes 2359300

commit v4 on v3

v4 whole, which is shorter than its diff:
```python
import functools

import jax
import jax.numpy as jnp
from jax import lax
from jax.experimental import pallas as pl
from jax.experimental.pallas import tpu as pltpu
from jax.sharding import PartitionSpec as P

radius = 0.3
MESH = pl.DeviceIdType.MESH
NT = (((1,), (1,)), ((), ()))
f32, bf16 = jnp.float32, jnp.bfloat16


def pointwise(gate_sum, up_sum, back_sum):
    sigmoid_gate = jax.nn.sigmoid(gate_sum)
    swish_gate = gate_sum * sigmoid_gate
    activation = (swish_gate * up_sum).astype(bf16)
    gate_delta = (
        back_sum * up_sum * sigmoid_gate * (1.0 + gate_sum * (1.0 - sigmoid_gate))
    ).astype(bf16)
    up_delta = (back_sum * swish_gate).astype(bf16)
    return (activation, gate_delta, up_delta)


def fold(x):
    rows, lanes = x.shape
    x = jnp.sum(x.reshape(rows // 8, 8, lanes), axis=0)
    return sum(x[:, i : i + 128] for i in range(0, lanes, 128))


def all_gather_plane(NY, NX, y, x, at_x, at_y, sibling, remote, arrive, leave):
    every = slice(None)

    def parts(order):
        if order == "xy":
            return (
                NX, NY, at_x, at_y,
                lambda core: (core, y, every),
                lambda i: (0, y, (x - i + NX) % NX),
                lambda core, i: (core, (y - i + NY) % NY, every),
            )
        return (
            NY, NX, at_y, at_x,
            lambda core: (core, every, x),
            lambda i: (0, (y - i + NY) % NY, x),
            lambda core, i: (core, every, (x - i + NX) % NX),
        )

    own = (0, y, x)

    def start(flow):
        view, order, ss, rs = flow
        n1, n2, first, second, line, one, lines = parts(order)
        for i in range(1, n1):
            remote(view(own), view(own), ss.at[0, i], rs.at[0, i], first(i)).start()

    def middle(flow):
        view, order, ss, rs = flow
        n1, n2, first, second, line, one, lines = parts(order)
        for i in range(1, n1):
            arrive(view(one(i)), ss.at[0, i], rs.at[0, i])
        for i in range(1, n2):
            remote(view(line(0)), view(line(0)), ss.at[1, i], rs.at[1, i], second(i)).start()
        remote(view(line(0)), view(line(1)), ss.at[2, 0], rs.at[2, 0], sibling).start()

    def across(flow):
        view, order, ss, rs = flow
        n1, n2, first, second, line, one, lines = parts(order)
        for i in range(1, n2):
            arrive(view(lines(0, i)), ss.at[1, i], rs.at[1, i])
            remote(
                view(lines(0, i)), view(lines(1, i)), ss.at[2, i], rs.at[2, i], sibling
            ).start()

    def finish(flow):
        view, order, ss, rs = flow
        n1, n2, first, second, line, one, lines = parts(order)
        for i in range(n2):
            arrive(view(lines(1, i)), ss.at[2, i], rs.at[2, i])

    def sent(flow):
        view, order, ss, rs = flow
        n1, n2, first, second, line, one, lines = parts(order)
        for i in range(1, n1):
            leave(view(own), ss.at[0, i], rs.at[0, i])
        for i in range(1, n2):
            leave(view(line(0)), ss.at[1, i], rs.at[1, i])
        for i in range(n2):
            leave(view(lines(0, i)), ss.at[2, i], rs.at[2, i])

    return start, middle, across, finish, sent


def powers(largest):
    scale = jnp.ones_like(largest)
    inverse = jnp.ones_like(largest)
    for e in (64, 32, 16, 8):
        over = largest >= 2.0**e
        under = largest < 2.0**-e
        down = jnp.where(over, 2.0**-e, jnp.where(under, 2.0**e, 1.0))
        up = jnp.where(over, 2.0**e, jnp.where(under, 2.0**-e, 1.0))
        largest, scale, inverse = largest * down, scale * down, inverse * up
    return scale, inverse


def kernel(
    NZ, NY, NX,
    features, cotangent, gate_master, up_master, down_master,
    deltas_out, tokens_t_out, targets_out,
    tok, tgt, stage, weights, tokens_t, part, outbox, inbox,
    kpart, kin, kown, kplane, gram, sums, steps, deltas, energy, energy_in,
    local_sem, out_sem, plane_s, plane_r, kz_s, kz_r, ch_s, ch_r, ag_s, ag_r, en_s, en_r,
):
    z, c, x = lax.axis_index("row"), lax.axis_index("col"), lax.axis_index("depth")
    y, k = c // 2, c % 2
    hidden = weights.shape[1]
    depth, tokens = tokens_t.shape
    own = hidden // NZ
    half = own // 2
    side = tokens // 2
    block = features.shape[0]
    span = tokens // 128

    def at_z(i):
        return ((z + i + NZ) % NZ, c, x)

    def at_y(i):
        return (z, ((y + i) % NY) * 2 + k, x)

    def at_x(i):
        return (z, c, (x + i) % NX)

    def at_pair(q):
        return (z, ((y + q // 2) % NY) * 2 + (k + q % 2) % 2, x)

    sibling = at_pair(1)

    def remote(src, dst, ssem, rsem, device):
        return pltpu.make_async_remote_copy(
            src_ref=src, dst_ref=dst, send_sem=ssem, recv_sem=rsem,
            device_id=device, device_id_type=MESH,
        )

    def arrive(dst, ssem, rsem):
        remote(dst, dst, ssem, rsem, sibling).wait_recv()

    def leave(src, ssem, rsem):
        remote(src, src, ssem, rsem, sibling).wait_send()

    masters = (gate_master, up_master, down_master)
    loads = [pltpu.make_async_copy(masters[m], stage.at[m], local_sem.at[m]) for m in range(3)]
    loads += [
        pltpu.make_async_copy(features, tok.at[0, y, x], local_sem.at[3]),
        pltpu.make_async_copy(cotangent, tgt.at[0, y, x], local_sem.at[4]),
    ]
    for load in loads[3:] + loads[:3]:
        load.start()

    barrier = pltpu.get_barrier_semaphore()
    partners = (
        [at_x(i) for i in range(1, NX)]
        + [at_pair(q) for q in range(1, 2 * NY)]
        + [at_z(i) for i in range(1, NZ)]
    )
    for device in partners:
        pl.semaphore_signal(barrier, inc=1, device_id=device, device_id_type=MESH)
    loads[3].wait()
    loads[4].wait()
    pl.semaphore_wait(barrier, len(partners))

    start, middle, across, finish, sent = all_gather_plane(
        NY, NX, y, x, at_x, at_y, sibling, remote, arrive, leave
    )

    flows_in = (
        (lambda where: tok.at[where], "xy", plane_s.at[0], plane_r.at[0]),
        (lambda where: tgt.at[where], "yx", plane_s.at[1], plane_r.at[1]),
    )
    flows_gram = tuple(
        (lambda where, g=g: kplane.at[(g, *where)], order, plane_s.at[2 + g], plane_r.at[2 + g])
        for g, order in enumerate(("xy", "yx"))
    )

    def run(step, flows):
        for flow in flows:
            step(flow)

    def prepare(m, transpose):
        loads[m].wait()
        rows = 128

        def body(i, total):
            r = pl.ds(pl.multiple_of(i * rows, rows), rows)
            piece = stage[m, r, :]
            if transpose:
                weights[m, :, r] = piece.astype(bf16).T
            else:
                weights[m, r, :] = piece.astype(bf16)
            return total + fold(piece * piece)

        return lax.fori_loop(0, hidden // rows, body, jnp.zeros((8, 128), f32))

    def hops(d, h):
        return NZ // 2 if d == h else NZ // 2 - 1

    signs = (1, -1)

    def chain_send(t, h, m):
        for d, sign in enumerate(signs):
            n = hops(d, h)
            if t >= n:
                continue
            owner = (z + sign * (n - t) + NZ) % NZ
            total = part[h, m, owner]
            if t > 0:
                arrive(inbox.at[d, t - 1, h, m], ch_s.at[d, t - 1, h, m], ch_r.at[d, t - 1, h, m])
                total = total + inbox[d, t - 1, h, m].astype(f32)
            outbox[d, t, h, m] = total.astype(outbox.dtype)
            remote(
                outbox.at[d, t, h, m], inbox.at[d, t, h, m],
                ch_s.at[d, t, h, m], ch_r.at[d, t, h, m], at_z(sign),
            ).start()

    def multiply(h, m):
        every = tok if m < 2 else tgt
        wide = hidden // 2
        for i in range(2):
            part[h, m, i * (NZ // 2) : (i + 1) * (NZ // 2)] = lax.dot_general(
                weights[m, i * wide : (i + 1) * wide, :],
                every[h].reshape(side, depth), NT, preferred_element_type=f32,
            ).reshape(NZ // 2, own, side)

    def loop3(f):
        def body(m, carry):
            f(m)
            return carry

        lax.fori_loop(0, 3, body, 0)

    def gram_partial():
        for g, every in enumerate((tok, tgt)):
            largest = jnp.max(jnp.abs(every[...].reshape(tokens // 16, 16, depth)), axis=0)
            largest = jnp.max(largest.astype(f32), axis=0, keepdims=True)
            largest = jnp.max(largest, axis=1, keepdims=True)
            scale, inverse = powers(largest)
            scaled = (every[0, y, x].astype(f32) * scale).astype(bf16)
            rows = lax.dot_general(
                scaled, every[...].reshape(tokens, depth), NT, preferred_element_type=f32
            ) * scale
            for j in range(span):
                kpart[g * span + j, 0:block] = rows[:, j * 128 : (j + 1) * 128]
                kpart[g * span + j, block : block + 4] = jnp.broadcast_to(scale, (4, 128))
                kpart[g * span + j, block + 4 : block + 8] = jnp.broadcast_to(inverse, (4, 128))
        for i in range(1, NZ):
            remote(
                kpart.at[(z + i) % NZ], kin.at[i], kz_s.at[0, i], kz_r.at[0, i], at_z(i)
            ).start()

    def gram_reduce():
        kin[0] = kpart[z]
        for i in range(1, NZ):
            arrive(kin.at[i], kz_s.at[0, i], kz_r.at[0, i])
        scale = functools.reduce(jnp.minimum, [kin[i, block : block + 1] for i in range(NZ)])
        total = jnp.zeros((block, 128), f32)
        for i in range(NZ):
            ratio = kin[i, block + 4 : block + 5] * scale
            total = total + kin[i, 0:block] * ratio * ratio
        kown[z, 0:block] = total
        kown[z, block : block + 8] = jnp.broadcast_to(
            functools.reduce(jnp.maximum, [kin[i, block + 4 : block + 5] for i in range(NZ)]),
            (8, 128),
        )
        for i in range(1, NZ):
            remote(kown.at[z], kown.at[z], kz_s.at[1, i], kz_r.at[1, i], at_z(i)).start()

    def gram_rows():
        for i in range(1, NZ):
            arrive(kown.at[(z - i + NZ) % NZ], kz_s.at[1, i], kz_r.at[1, i])
        first = (y * NX + x) * block
        rows = lax.broadcasted_iota(jnp.int32, (block, 128), 0)
        columns = lax.broadcasted_iota(jnp.int32, (block, 128), 1)
        for g in range(2):
            rest = []
            for j in range(span):
                piece = kown[g * span + j, 0:block]
                high = piece.astype(bf16)
                kplane[g, 0, y, x, j] = high
                low = jnp.where(columns + j * 128 == rows + first, piece - high.astype(f32), 0.0)
                rest.append(jnp.sum(low, axis=0, keepdims=True))
            rest.append(jnp.zeros((block - span, 128), f32))
            kplane[g, 0, y, x, span] = jnp.concatenate(rest, axis=0).astype(bf16)

    run(start, flows_in)
    weight_energy = prepare(0, True)
    run(middle, flows_in)
    weight_energy += prepare(1, True)
    weight_energy += prepare(2, False)
    across(flows_in[0])
    for m in range(2):
        multiply(0, m)
        chain_send(0, 0, m)
    across(flows_in[1])
    multiply(0, 2)
    chain_send(0, 0, 2)
    run(finish, flows_in)
    gram_partial()
    for m in range(3):
        multiply(1, m)
    for m in range(3):
        chain_send(1, 0, m)
    gram_reduce()
    for m in range(3):
        chain_send(0, 1, m)
    for m in range(3):
        chain_send(2, 0, m)
    gram_rows()
    run(start, flows_gram)

    tokens_t[...] = tok[...].reshape(tokens, depth).T
    copies = [
        pltpu.make_async_copy(tokens_t, tokens_t_out, local_sem.at[0]),
        pltpu.make_async_copy(tgt, targets_out, local_sem.at[1]),
    ]
    for copy in copies:
        copy.start()

    for m in range(3):
        chain_send(1, 1, m)
    run(middle, flows_gram)
    for m in range(3):
        chain_send(3, 0, m)
        chain_send(2, 1, m)
    run(across, flows_gram)
    for m in range(3):
        chain_send(3, 1, m)
    run(finish, flows_gram)

    rest = []
    for g in range(2):
        low = [None] * span
        for core in range(2):
            r = slice(core * side, (core + 1) * side)
            lows = kplane[g, core, :, :, span].reshape(side // block, block, 128)
            lows = jnp.sum(lows.astype(f32), axis=0)
            for j in range(span):
                at = (j + core * span // 2) % span
                gram[g, r, at * 128 : (at + 1) * 128] = kplane[g, core, :, :, j].reshape(side, 128)
                low[at] = lows[j : j + 1] if core == 0 else low[at] + lows[j : j + 1]
        rest.append(jnp.concatenate(low, axis=1))
    inverse_tok = kown[0, block : block + 1, 0:1]
    inverse_tgt = kown[span, block : block + 1, 0:1]

    def chain_last(m):
        for h in range(2):
            total = part[h, m, z]
            for d in range(2):
                last = hops(d, h) - 1
                arrive(inbox.at[d, last, h, m], ch_s.at[d, last, h, m], ch_r.at[d, last, h, m])
                total = total + inbox[d, last, h, m].astype(f32)
            sums[m, :, h * side : (h + 1) * side] = total

    loop3(chain_last)

    gate_sum, up_sum, back_sum = sums[0], sums[1], sums[2]
    activation, gate_delta, up_delta = pointwise(gate_sum, up_sum, back_sum)

    def gram_dot(delta, g, inverse):
        product = jnp.dot(delta, gram[g], preferred_element_type=f32)
        return (product + delta.astype(f32) * rest[g]) * inverse

    both = gram_dot(jnp.concatenate([gate_delta, up_delta], axis=0), 0, inverse_tok)
    back_step = gram_dot(activation, 1, inverse_tgt)
    gate_step, up_step = both[:own], both[own:]
    steps[0], steps[1], steps[2] = gate_step, up_step, back_step
    gradient_energy = (
        fold(gate_delta.astype(f32) * inverse_tok * gate_step)
        + fold(up_delta.astype(f32) * inverse_tok * up_step)
        + fold(activation.astype(f32) * inverse_tgt * back_step)
    )
    both_energy = jnp.concatenate(
        [
            jnp.sum(weight_energy, axis=0, keepdims=True),
            jnp.sum(gradient_energy, axis=0, keepdims=True),
            jnp.zeros((6, 128), f32),
        ],
        axis=0,
    )
    spans = ((NX, at_x), (2 * NY, at_pair), (NZ, at_z))
    for axis, (count, where) in enumerate(spans):
        energy[axis] = both_energy
        for q in range(1, count):
            remote(
                energy.at[axis], energy_in.at[axis, q], en_s.at[axis, q], en_r.at[axis, q], where(q)
            ).start()
        for q in range(1, count):
            arrive(energy_in.at[axis, q], en_s.at[axis, q], en_r.at[axis, q])
            both_energy = both_energy + energy_in[axis, q]
    totals = jnp.sum(both_energy, axis=1, keepdims=True)
    step_scale = (
        radius * jnp.sqrt(totals[0:1]) / jnp.sqrt(jnp.maximum(totals[1:2], 0.0) + 1e-06)
    )
    step_tok, step_tgt = step_scale * inverse_tok, step_scale * inverse_tgt

    second = pointwise(
        sums[0] + step_tok * steps[0],
        sums[1] + step_tok * steps[1],
        sums[2] + step_tgt * steps[2],
    )

    def to_hbm(m, owner, h):
        return pltpu.make_async_copy(
            deltas.at[m, owner, h], deltas_out.at[m, owner, h], out_sem.at[m, owner, h]
        )

    def spread(t, m):
        for h in range(2):
            for d, sign in enumerate(signs):
                n = hops(d, h)
                owner = (z - sign * t + NZ) % NZ
                there = deltas.at[m, owner, h]
                if 0 < t <= n:
                    arrive(there, ag_s.at[d, t - 1, m, h], ag_r.at[d, t - 1, m, h])
                if t < n:
                    remote(
                        there, there, ag_s.at[d, t, m, h], ag_r.at[d, t, m, h], at_z(sign)
                    ).start()
                if 0 < t <= n:
                    to_hbm(m, owner, h).start()

    for m in range(3):
        deltas[m, z] = second[m].reshape(2, half, tokens)
        spread(0, m)

    def own_to_hbm(m):
        for h in range(2):
            to_hbm(m, z, h).start()

    loop3(own_to_hbm)

    for flow in flows_in + flows_gram:
        sent(flow)
    for i in range(1, NZ):
        leave(kpart.at[(z + i) % NZ], kz_s.at[0, i], kz_r.at[0, i])
        leave(kown.at[z], kz_s.at[1, i], kz_r.at[1, i])
    for axis, (count, where) in enumerate(spans):
        for q in range(1, count):
            leave(energy.at[axis], en_s.at[axis, q], en_r.at[axis, q])

    def chains_sent(m):
        for d in range(2):
            for h in range(2):
                for t in range(hops(d, h)):
                    leave(outbox.at[d, t, h, m], ch_s.at[d, t, h, m], ch_r.at[d, t, h, m])

    loop3(chains_sent)
    for copy in copies:
        copy.wait()

    for t in range(1, NZ // 2 + 1):
        loop3(functools.partial(spread, t))

    def spread_sent(m):
        for d, sign in enumerate(signs):
            for h in range(2):
                for t in range(hops(d, h)):
                    leave(
                        deltas.at[m, (z - sign * t + NZ) % NZ, h],
                        ag_s.at[d, t, m, h], ag_r.at[d, t, m, h],
                    )
        for owner in range(NZ):
            for h in range(2):
                to_hbm(m, owner, h).wait()

    loop3(spread_sent)


def gradients(tokens_t, deltas, targets, gate_out, up_out, down_out):
    gate_out[...] = lax.dot_general(
        tokens_t[...], deltas[1], NT, preferred_element_type=f32
    ).astype(bf16)
    up_out[...] = lax.dot_general(
        tokens_t[...], deltas[2], NT, preferred_element_type=f32
    ).astype(bf16)
    down_out[...] = jnp.dot(deltas[0], targets[...], preferred_element_type=f32).astype(bf16)


def shards(NZ, NY, NX, features, cotangent, gate_master, up_master, down_master):
    block, depth = features.shape
    hidden = gate_master.shape[1]
    tokens = block * NY * 2 * NX
    half = hidden // NZ // 2
    hops = NZ // 2
    span = tokens // 128
    vmem = pltpu.VMEM
    dma = pltpu.SemaphoreType.DMA
    plane = (2, NY, NX)
    scratch = [
        vmem(plane + (block, depth), bf16),
        vmem(plane + (block, depth), bf16),
        vmem((3, depth, hidden), f32),
        vmem((3, hidden, depth), bf16),
        vmem((depth, tokens), bf16),
        vmem((2, 3, NZ, 2 * half, tokens // 2), f32),
        vmem((2, hops, 2, 3, 2 * half, tokens // 2), bf16),
        vmem((2, hops, 2, 3, 2 * half, tokens // 2), bf16),
        vmem((NZ, block + 8, 128), f32),
        vmem((NZ, block + 8, 128), f32),
        vmem((NZ, block + 8, 128), f32),
        vmem((2,) + plane + (span + 1, block, 128), bf16),
        vmem((2, tokens, tokens), bf16),
        vmem((3, 2 * half, tokens), f32),
        vmem((3, 2 * half, tokens), f32),
        vmem((3, NZ, 2, half, tokens), bf16),
        vmem((3, 8, 128), f32),
        vmem((3, max(NZ, 2 * NY), 8, 128), f32),
        dma((5,)),
        dma((3, NZ, 2)),
        dma((4, 3, max(NX, NY))),
        dma((4, 3, max(NX, NY))),
        dma((2, NZ)),
        dma((2, NZ)),
        dma((2, hops, 2, 3)),
        dma((2, hops, 2, 3)),
        dma((2, hops, 3, 2)),
        dma((2, hops, 3, 2)),
        dma((3, max(NZ, 2 * NY))),
        dma((3, max(NZ, 2 * NY))),
    ]
    away = pl.BlockSpec(memory_space=pl.ANY)
    deltas, tokens_t, targets = pl.pallas_call(
        functools.partial(kernel, NZ, NY, NX),
        out_shape=(
            jax.ShapeDtypeStruct((3, NZ, 2, half, tokens), bf16),
            jax.ShapeDtypeStruct((depth, tokens), bf16),
            jax.ShapeDtypeStruct(plane + (block, depth), bf16),
        ),
        in_specs=[away] * 5,
        out_specs=(away, away, away),
        scratch_shapes=scratch,
        compiler_params=pltpu.CompilerParams(
            collective_id=0, has_side_effects=True, vmem_limit_bytes=56 * 1024 * 1024
        ),
        cost_estimate=pl.CostEstimate(
            flops=2 * 3 * hidden * depth * tokens,
            bytes_accessed=4 * 3 * hidden * depth,
            transcendentals=0,
        ),
    )(features, cotangent, gate_master, up_master, down_master)
    tile = hidden // 3
    return pl.pallas_call(
        gradients,
        grid=(hidden // tile,),
        out_shape=(
            jax.ShapeDtypeStruct((depth, hidden), bf16),
            jax.ShapeDtypeStruct((depth, hidden), bf16),
            jax.ShapeDtypeStruct((hidden, depth), bf16),
        ),
        in_specs=[
            pl.BlockSpec((depth, tokens), lambda i: (0, 0)),
            pl.BlockSpec((3, tile, tokens), lambda i: (0, i, 0)),
            pl.BlockSpec((tokens, depth), lambda i: (0, 0)),
        ],
        out_specs=(
            pl.BlockSpec((depth, tile), lambda i: (0, i)),
            pl.BlockSpec((depth, tile), lambda i: (0, i)),
            pl.BlockSpec((tile, depth), lambda i: (i, 0)),
        ),
        compiler_params=pltpu.CompilerParams(vmem_limit_bytes=60 * 1024 * 1024),
        cost_estimate=pl.CostEstimate(
            flops=2 * 3 * hidden * depth * tokens,
            bytes_accessed=2 * (5 * hidden * tokens + 3 * hidden * depth),
            transcendentals=0,
        ),
    )(tokens_t, deltas.reshape(3, hidden, tokens), targets.reshape(tokens, depth))


def solution(mesh):
    placed = (
        P(("col", "depth"), "row"),
        P(("col", "depth"), "row"),
        P("row", ("col", "depth")),
        P("row", ("col", "depth")),
        P(("col", "depth"), "row"),
    )
    return jax.shard_map(
        functools.partial(shards, mesh.shape["row"], mesh.shape["col"] // 2, mesh.shape["depth"]),
        mesh=mesh,
        in_specs=placed,
        out_specs=(
            P("row", ("col", "depth")),
            P("row", ("col", "depth")),
            P(("col", "depth"), "row"),
        ),
        check_vma=False,
    )
```

time: 104 us -> 95.4 us (0.917); the launches traced: 102 us -> 94.8 us
  local copies, waits for them, and re-layouts: 3.92 us -> 0 us
  Pallas kernels: 97.3 us -> 94.1 us
    pallas_call x1, Pallas kernels: 93.8 us -> 88.5 us  [shards(): pl.pallas_call(functools.partial(kernel, NZ, NY, NX), out_shape=(jax.Shap...]
    unnamed x6 -> x0, local copies, waits for them, and re-layouts: 3.92 us -> none
    pallas_call x1, Pallas kernels: 3.49 us -> 5.57 us  [shards(): pl.pallas_call(gradients, grid=(hidden // tile,), out_shape=(jax.ShapeDty...]
where the time goes in v4:
time: 95.4 us; the launch traced here: 94.8 us
  Pallas kernels  94.1 us (99%)
    pallas_call x1, Pallas kernels, shards(): pl.pallas_call(functools.partial(kernel, NZ, NY, NX), out_shape=(jax.Shap...  88.5 us
    pallas_call x1, Pallas kernels, shards(): pl.pallas_call(gradients, grid=(hidden // tile,), out_shape=(jax.ShapeDty...  5.57 us

profile of v4, /device:TPU:2, one launch (start us, length us, event | category | flops | bytes accessed | tf_op | source)
XLA Modules:
  0.0 94.8 jit_solution(6125809869777288545)
XLA Ops:
  0.6 88.5 %shard_map.76 = (bf16[3,8,2,48,512]{4,3,2,1,0:T(8,128)(2,1)}, bf16[768,512]{1,0:T(8,128)(2,1)}, bf16[2,4,4,16,768]{4,3,2,1,0:T(8,128)(2,1)}) custom-call(bf16[16,768]{1,0:T(8,128)(2,1)} %features.1, bf16[16,768]{1,0:T(8,128)(2,1)} %cotangent.1, f32[768,768]{1,0:T(8,128)} %gate_master.1, f32[768,768]{1,0:T(8,128)} %up_master.1, f32[768,768]{1,0:T(8,128)} %down_master.1), custom_call_target="tpu_custom_call" | custom-call | flops 1811939328 | bytes 7077888 | tf_op jit(solution)/shard_map/pallas_call | solution.py:532
  89.2 5.6 %shard_map.77 = (bf16[768,768]{1,0:T(8,128)(2,1)}, bf16[768,768]{1,0:T(8,128)(2,1)}, bf16[768,768]{1,0:T(8,128)(2,1)}) custom-call(bf16[768,512]{1,0:T(8,128)(2,1)} %get-tuple-element.6.tokens_t, bf16[3,768,512]{2,1,0:T(8,128)(2,1)} %bitcast.2, bf16[512,768]{1,0:T(8,128)(2,1)} %bitcast.3), custom_call_target="tpu_custom_call" | custom-call | flops 1811939328 | bytes 7471104 | tf_op jit(solution)/shard_map/pallas_call | solution.py:552

commit v5 on v4

--- a/solution.py
+++ b/solution.py
@@ -77,8 +77,12 @@
     def finish(flow):
         view, order, ss, rs = flow
         n1, n2, first, second, line, one, lines = parts(order)
-        for i in range(n2):
+        for i in range(1, n2):
             arrive(view(lines(1, i)), ss.at[2, i], rs.at[2, i])
+
+    def sibling_line(flow):
+        view, order, ss, rs = flow
+        arrive(view(parts(order)[4](1)), ss.at[2, 0], rs.at[2, 0])
 
     def sent(flow):
         view, order, ss, rs = flow
@@ -90,7 +94,13 @@
         for i in range(n2):
             leave(view(lines(0, i)), ss.at[2, i], rs.at[2, i])
 
-    return start, middle, across, finish, sent
+    return start, middle, across, sibling_line, finish, sent
+
+
+def peak_of(x):
+    rows, lanes = x.shape
+    x = jnp.max(jnp.abs(x).reshape(rows // 8, 8, lanes), axis=0)
+    return functools.reduce(jnp.maximum, [x[:, i : i + 128] for i in range(0, lanes, 128)])
 
 
 def powers(largest):
@@ -110,7 +120,7 @@
     features, cotangent, gate_master, up_master, down_master,
     deltas_out, tokens_t_out, targets_out,
     tok, tgt, stage, weights, tokens_t, part, outbox, inbox,
-    kpart, kin, kown, kplane, gram, sums, steps, deltas, energy, energy_in,
+    kpart, kin, kown, heads, codes, kplane, gram, vectors, sums, steps, deltas, energy, energy_in,
     local_sem, out_sem, plane_s, plane_r, kz_s, kz_r, ch_s, ch_r, ag_s, ag_r, en_s, en_r,
 ):
     z, c, x = lax.axis_index("row"), lax.axis_index("col"), lax.axis_index("depth")
@@ -170,7 +180,7 @@
     loads[4].wait()
     pl.semaphore_wait(barrier, len(partners))
 
-    start, middle, across, finish, sent = all_gather_plane(
+    start, middle, across, sibling_line, finish, sent = all_gather_plane(
         NY, NX, y, x, at_x, at_y, sibling, remote, arrive, leave
     )
 
@@ -198,14 +208,29 @@
                 weights[m, :, r] = piece.astype(bf16).T
             else:
                 weights[m, r, :] = piece.astype(bf16)
-            return total + fold(piece * piece)
-
-        return lax.fori_loop(0, hidden // rows, body, jnp.zeros((8, 128), f32))
+            energy_now, peak = total
+            return energy_now + fold(piece * piece), jnp.maximum(peak, peak_of(piece))
+
+        zero = jnp.zeros((8, 128), f32)
+        return lax.fori_loop(0, hidden // rows, body, (zero, zero))
 
     def hops(d, h):
         return NZ // 2 if d == h else NZ // 2 - 1
 
     signs = (1, -1)
+
+    def encode(total, m):
+        total = total * codes[m : m + 1, 0:1]
+        return (total * jnp.abs(total)).astype(bf16)
+
+    def decode(square, m):
+        square = square.astype(f32)
+        root = square * lax.rsqrt(jnp.maximum(jnp.abs(square), 1e-37))
+        return root * codes[4 + m : 5 + m, 0:1]
+
+    def received(d, t, h, m):
+        arrive(inbox.at[d, t, h, m], ch_s.at[d, t, h, m], ch_r.at[d, t, h, m])
+        return decode(inbox[d, t, h, m], m) if t >= 2 else inbox[d, t, h, m].astype(f32)
 
     def chain_send(t, h, m):
         for d, sign in enumerate(signs):
@@ -215,9 +240,8 @@
             owner = (z + sign * (n - t) + NZ) % NZ
             total = part[h, m, owner]
             if t > 0:
-                arrive(inbox.at[d, t - 1, h, m], ch_s.at[d, t - 1, h, m], ch_r.at[d, t - 1, h, m])
-                total = total + inbox[d, t - 1, h, m].astype(f32)
-            outbox[d, t, h, m] = total.astype(outbox.dtype)
+                total = total + received(d, t - 1, h, m)
+            outbox[d, t, h, m] = encode(total, m) if t >= 2 else total.astype(bf16)
             remote(
                 outbox.at[d, t, h, m], inbox.at[d, t, h, m],
                 ch_s.at[d, t, h, m], ch_r.at[d, t, h, m], at_z(sign),
@@ -240,19 +264,26 @@
         lax.fori_loop(0, 3, body, 0)
 
     def gram_partial():
+        first_lanes = lax.broadcasted_iota(jnp.int32, (1, 128), 1) < 64
+        head, scales = [], []
+        for peak in (peak_of(tok[0].reshape(side, depth).astype(f32)),
+                     peak_of(tgt[0].reshape(side, depth).astype(f32)), *weight_peaks):
+            peak = jnp.max(jnp.max(peak, axis=0, keepdims=True), axis=1, keepdims=True)
+            scale, inverse = powers(peak)
+            scales.append(scale)
+            head.append(jnp.where(first_lanes, inverse, scale))
+        head = jnp.concatenate(head + [jnp.ones((3, 128), f32)], axis=0)
         for g, every in enumerate((tok, tgt)):
-            largest = jnp.max(jnp.abs(every[...].reshape(tokens // 16, 16, depth)), axis=0)
-            largest = jnp.max(largest.astype(f32), axis=0, keepdims=True)
-            largest = jnp.max(largest, axis=1, keepdims=True)
-            scale, inverse = powers(largest)
-            scaled = (every[0, y, x].astype(f32) * scale).astype(bf16)
+            pair = jnp.concatenate(
+                [(every[0, y, x].astype(f32) * scales[g]).astype(bf16), every[1, y, x]], axis=0
+            )
             rows = lax.dot_general(
-                scaled, every[...].reshape(tokens, depth), NT, preferred_element_type=f32
-            ) * scale
-            for j in range(span):
-                kpart[g * span + j, 0:block] = rows[:, j * 128 : (j + 1) * 128]
-                kpart[g * span + j, block : block + 4] = jnp.broadcast_to(scale, (4, 128))
-                kpart[g * span + j, block + 4 : block + 8] = jnp.broadcast_to(inverse, (4, 128))
+                pair, every[0].reshape(side, depth), NT, preferred_element_type=f32
+            ) * scales[g]
+            for p in range(span):
+                r, j = p // (span // 2) * block, p % (span // 2) * 128
+                kpart[g * span + p, 0:block] = rows[r : r + block, j : j + 128]
+                kpart[g * span + p, block : block + 8] = head
         for i in range(1, NZ):
             remote(
                 kpart.at[(z + i) % NZ], kin.at[i], kz_s.at[0, i], kz_r.at[0, i], at_z(i)
@@ -262,16 +293,27 @@
         kin[0] = kpart[z]
         for i in range(1, NZ):
             arrive(kin.at[i], kz_s.at[0, i], kz_r.at[0, i])
-        scale = functools.reduce(jnp.minimum, [kin[i, block : block + 1] for i in range(NZ)])
+        inverses = functools.reduce(jnp.maximum, [kin[i, block : block + 8] for i in range(NZ)])
+        scales = functools.reduce(jnp.minimum, [kin[i, block : block + 8] for i in range(NZ)])
+        heads[0], heads[1] = inverses, scales
+        for m in range(3):
+            g, w = m // 2, 2 + m
+            code = scales[g : g + 1, 64:65] * scales[w : w + 1, 64:65]
+            back = inverses[g : g + 1, 0:1] * inverses[w : w + 1, 0:1]
+            code = jnp.clip(code, 2.0**-100, 2.0**90) * 2.0**30
+            back = jnp.clip(back, 2.0**-90, 2.0**100) * 2.0**-30
+            codes[m : m + 1] = jnp.broadcast_to(code, (1, 128))
+            codes[4 + m : 5 + m] = jnp.broadcast_to(back, (1, 128))
+        is_tok = z < span
+        scale = jnp.where(is_tok, scales[0:1, 64:65], scales[1:2, 64:65])
+        squared = z % span < span // 2
         total = jnp.zeros((block, 128), f32)
         for i in range(NZ):
-            ratio = kin[i, block + 4 : block + 5] * scale
-            total = total + kin[i, 0:block] * ratio * ratio
-        kown[z, 0:block] = total
-        kown[z, block : block + 8] = jnp.broadcast_to(
-            functools.reduce(jnp.maximum, [kin[i, block + 4 : block + 5] for i in range(NZ)]),
-            (8, 128),
-        )
+            ratio = scale * jnp.where(
+                is_tok, kin[i, block : block + 1, 0:1], kin[i, block + 1 : block + 2, 0:1]
+            )
+            total = total + kin[i, 0:block] * ratio * jnp.where(squared, ratio, 1.0)
+        kown[z] = total
         for i in range(1, NZ):
             remote(kown.at[z], kown.at[z], kz_s.at[1, i], kz_r.at[1, i], at_z(i)).start()
 
@@ -283,197 +325,258 @@
         columns = lax.broadcasted_iota(jnp.int32, (block, 128), 1)
         for g in range(2):
             rest = []
-            for j in range(span):
-                piece = kown[g * span + j, 0:block]
+            for p in range(span):
+                piece = kown[g * span + p]
                 high = piece.astype(bf16)
-                kplane[g, 0, y, x, j] = high
-                low = jnp.where(columns + j * 128 == rows + first, piece - high.astype(f32), 0.0)
-                rest.append(jnp.sum(low, axis=0, keepdims=True))
-            rest.append(jnp.zeros((block - span, 128), f32))
+                kplane[g, 0, y, x, p] = high
+                if p < span // 2:
+                    low = jnp.where(
+                        columns + p * 128 == rows + first, piece - high.astype(f32), 0.0
+                    )
+                    rest.append(jnp.sum(low, axis=0, keepdims=True))
+            rest.append(jnp.broadcast_to(heads[0, g : g + 1, 0:1], (1, 128)))
+            rest.append(jnp.zeros((block - span // 2 - 1, 128), f32))
             kplane[g, 0, y, x, span] = jnp.concatenate(rest, axis=0).astype(bf16)
 
     run(start, flows_in)
-    weight_energy = prepare(0, True)
+    weight_energy, gate_peak = prepare(0, True)
     run(middle, flows_in)
-    weight_energy += prepare(1, True)
-    weight_energy += prepare(2, False)
-    across(flows_in[0])
-    for m in range(2):
-        multiply(0, m)
-        chain_send(0, 0, m)
-    across(flows_in[1])
-    multiply(0, 2)
-    chain_send(0, 0, 2)
-    run(finish, flows_in)
-    gram_partial()
-    for m in range(3):
-        multiply(1, m)
-    for m in range(3):
-        chain_send(1, 0, m)
-    gram_reduce()
-    for m in range(3):
-        chain_send(0, 1, m)
-    for m in range(3):
-        chain_send(2, 0, m)
-    gram_rows()
-    run(start, flows_gram)
-
-    tokens_t[...] = tok[...].reshape(tokens, depth).T
-    copies = [
-        pltpu.make_async_copy(tokens_t, tokens_t_out, local_sem.at[0]),
-        pltpu.make_async_copy(tgt, targets_out, local_sem.at[1]),
-    ]
-    for copy in copies:
-        copy.start()
-
-    for m in range(3):
-        chain_send(1, 1, m)
-    run(middle, flows_gram)
-    for m in range(3):
-        chain_send(3, 0, m)
-        chain_send(2, 1, m)
-    run(across, flows_gram)
-    for m in range(3):
-        chain_send(3, 1, m)
-    run(finish, flows_gram)
-
-    rest = []
-    for g in range(2):
-        low = [None] * span
-        for core in range(2):
-            r = slice(core * side, (core + 1) * side)
-            lows = kplane[g, core, :, :, span].reshape(side // block, block, 128)
-            lows = jnp.sum(lows.astype(f32), axis=0)
-            for j in range(span):
-                at = (j + core * span // 2) % span
-                gram[g, r, at * 128 : (at + 1) * 128] = kplane[g, core, :, :, j].reshape(side, 128)
-                low[at] = lows[j : j + 1] if core == 0 else low[at] + lows[j : j + 1]
-        rest.append(jnp.concatenate(low, axis=1))
-    inverse_tok = kown[0, block : block + 1, 0:1]
-    inverse_tgt = kown[span, block : block + 1, 0:1]
-
-    def chain_last(m):
-        for h in range(2):
-            total = part[h, m, z]
-            for d in range(2):
-                last = hops(d, h) - 1
-                arrive(inbox.at[d, last, h, m], ch_s.at[d, last, h, m], ch_r.at[d, last, h, m])
-                total = total + inbox[d, last, h, m].astype(f32)
-            sums[m, :, h * side : (h + 1) * side] = total
-
-    loop3(chain_last)
-
-    gate_sum, up_sum, back_sum = sums[0], sums[1], sums[2]
-    activation, gate_delta, up_delta = pointwise(gate_sum, up_sum, back_sum)
-
-    def gram_dot(delta, g, inverse):
-        product = jnp.dot(delta, gram[g], preferred_element_type=f32)
-        return (product + delta.astype(f32) * rest[g]) * inverse
-
-    both = gram_dot(jnp.concatenate([gate_delta, up_delta], axis=0), 0, inverse_tok)
-    back_step = gram_dot(activation, 1, inverse_tgt)
-    gate_step, up_step = both[:own], both[own:]
-    steps[0], steps[1], steps[2] = gate_step, up_step, back_step
-    gradient_energy = (
-        fold(gate_delta.astype(f32) * inverse_tok * gate_step)
-        + fold(up_delta.astype(f32) * inverse_tok * up_step)
-        + fold(activation.astype(f32) * inverse_tgt * back_step)
-    )
-    both_energy = jnp.concatenate(
-        [
-            jnp.sum(weight_energy, axis=0, keepdims=True),
-            jnp.sum(gradient_energy, axis=0, keepdims=True),
-            jnp.zeros((6, 128), f32),
-        ],
-        axis=0,
-    )
-    spans = ((NX, at_x), (2 * NY, at_pair), (NZ, at_z))
-    for axis, (count, where) in enumerate(spans):
-        energy[axis] = both_energy
-        for q in range(1, count):
-            remote(
-                energy.at[axis], energy_in.at[axis, q], en_s.at[axis, q], en_r.at[axis, q], where(q)
-            ).start()
-        for q in range(1, count):
-            arrive(energy_in.at[axis, q], en_s.at[axis, q], en_r.at[axis, q])
-            both_energy = both_energy + energy_in[axis, q]
-    totals = jnp.sum(both_energy, axis=1, keepdims=True)
-    step_scale = (
-        radius * jnp.sqrt(totals[0:1]) / jnp.sqrt(jnp.maximum(totals[1:2], 0.0) + 1e-06)
-    )
-    step_tok, step_tgt = step_scale * inverse_tok, step_scale * inverse_tgt
-
-    second = pointwise(
-        sums[0] + step_tok * steps[0],
-        sums[1] + step_tok * steps[1],
-        sums[2] + step_tgt * steps[2],
-    )
-
-    def to_hbm(m, owner, h):
-        return pltpu.make_async_copy(
-            deltas.at[m, owner, h], deltas_out.at[m, owner, h], out_sem.at[m, owner, h]
-        )
+    more, up_peak = prepare(1, True)
+    last, down_peak = prepare(2, False)
+    weight_energy = weight_energy + more + last
+    weight_peaks = (gate_peak, up_peak, down_peak)
+    copies = []
+
+    def transposed():
+        tokens_t[...] = tok[...].reshape(tokens, depth).T
+        copies.append(pltpu.make_async_copy(tokens_t, tokens_t_out, local_sem.at[0]))
+        copies.append(pltpu.make_async_copy(tgt, targets_out, local_sem.at[1]))
+        for copy in copies:
+            copy.start()
+
+    def gram_whole():
+        for g in range(2):
+            low, back = [], []
+            for core in range(2):
+                for p in range(span):
+                    first = (core + p // (span // 2)) % 2 * side
+                    j = core * side + p % (span // 2) * 128
+                    gram[g, first : first + side, j : j + 128] = kplane[
+                        g, core, :, :, p
+                    ].reshape(side, 128)
+                lows = kplane[g, core, :, :, span].reshape(side // block, block, 128).astype(f32)
+                back.append(lows[0, span // 2 : span // 2 + 1])
+                lows = jnp.sum(lows, axis=0)
+                low += [lows[j : j + 1] for j in range(span // 2)]
+            vectors[g, 0:1] = jnp.concatenate(low, axis=1)
+            vectors[2 + g, 0:1] = jnp.concatenate(
+                [b for b in back for _ in range(span // 2)], axis=1
+            )
 
     def spread(t, m):
         for h in range(2):
             for d, sign in enumerate(signs):
                 n = hops(d, h)
                 owner = (z - sign * t + NZ) % NZ
-                there = deltas.at[m, owner, h]
+                there = sums.at[m, owner, h]
                 if 0 < t <= n:
                     arrive(there, ag_s.at[d, t - 1, m, h], ag_r.at[d, t - 1, m, h])
                 if t < n:
                     remote(
                         there, there, ag_s.at[d, t, m, h], ag_r.at[d, t, m, h], at_z(sign)
                     ).start()
-                if 0 < t <= n:
-                    to_hbm(m, owner, h).start()
-
+
+    def chain_last(m):
+        halves = []
+        for h in range(2):
+            total = part[h, m, z]
+            for d in range(2):
+                total = total + received(d, hops(d, h) - 1, h, m)
+            halves.append(total)
+        total = jnp.concatenate(halves, axis=1)
+        sums[m, z] = encode(total, m).reshape(2, half, tokens)
+        spread(0, m)
+
+    def sums_of(owner):
+        return [decode(sums[m, owner].reshape(own, tokens), m) for m in range(3)]
+
+    def gram_dot(delta, g):
+        own_half = lax.broadcasted_iota(jnp.int32, (1, tokens), 1) < side
+        plain = delta.astype(f32)
+        scaled = plain * vectors[2 + g, 0:1]
+        halves = []
+        for core in range(2):
+            mixed = jnp.where(own_half == (core == 0), scaled, plain).astype(bf16)
+            halves.append(
+                jnp.dot(
+                    mixed, gram[g, :, core * side : (core + 1) * side], preferred_element_type=f32
+                )
+            )
+        return scaled, jnp.concatenate(halves, axis=1) + scaled * vectors[g, 0:1]
+
+    def first_pass(owner, own_units=False):
+        activation, gate_delta, up_delta = pointwise(*sums_of(owner))
+        scaled, both = gram_dot(jnp.concatenate([gate_delta, up_delta], axis=0), 0)
+        back_scaled, back = gram_dot(activation, 1)
+        steps[0, owner], steps[1, owner], steps[2, owner] = both[:own], both[own:], back
+        if own_units:
+            return fold(scaled * both) + fold(back_scaled * back)
+
+    def to_hbm(m, owner):
+        return pltpu.make_async_copy(deltas.at[m, owner], deltas_out.at[m, owner], out_sem.at[m, owner])
+
+    def second_pass(owner):
+        parts = [
+            total + vectors[4 if m < 2 else 5, 0:1] * steps[m, owner]
+            for m, total in enumerate(sums_of(owner))
+        ]
+        for m, part_m in enumerate(pointwise(*parts)):
+            deltas[m, owner] = part_m
+            to_hbm(m, owner).start()
+
+    def at_distance(f, t):
+        if t == 0 or 2 * t == NZ:
+            f((z + t) % NZ)
+            return
+
+        def body(i, carry):
+            f((z + (1 - 2 * i) * t + NZ) % NZ)
+            return carry
+
+        lax.fori_loop(0, 2, body, 0)
+
+    spans = ((NX, at_x), (2 * NY, at_pair), (NZ, at_z))
+
+    def energy_send(i, tile):
+        energy[i] = tile
+        count, where = spans[i]
+        for q in range(1, count):
+            remote(
+                energy.at[i], energy_in.at[i, q], en_s.at[i, q], en_r.at[i, q], where(q)
+            ).start()
+
+    def energy_own():
+        gradient_energy = first_pass(z, own_units=True)
+        energy_send(
+            0,
+            jnp.concatenate(
+                [
+                    jnp.sum(weight_energy, axis=0, keepdims=True),
+                    jnp.sum(gradient_energy, axis=0, keepdims=True),
+                    jnp.zeros((6, 128), f32),
+                ],
+                axis=0,
+            ),
+        )
+
+    def energy_wait(i):
+        tile = energy[i]
+        for q in range(1, spans[i][0]):
+            arrive(energy_in.at[i, q], en_s.at[i, q], en_r.at[i, q])
+            tile = tile + energy_in[i, q]
+        if i + 1 < len(spans):
+            energy_send(i + 1, tile)
+            return
+        totals = jnp.sum(tile, axis=1, keepdims=True)
+        step_scale = (
+            radius * jnp.sqrt(totals[0:1]) / jnp.sqrt(jnp.maximum(totals[1:2], 0.0) + 1e-06)
+        )
+        for g in range(2):
+            vectors[4 + g, 0:1] = step_scale * vectors[2 + g, 0:1]
+
+    def early_sent():
+        for flow in flows_in + flows_gram:
+            sent(flow)
+        for i in range(1, NZ):
+            leave(kpart.at[(z + i) % NZ], kz_s.at[0, i], kz_r.at[0, i])
+            leave(kown.at[z], kz_s.at[1, i], kz_r.at[1, i])
+
+        def chains_sent(m):
+            for d in range(2):
+                for h in range(2):
+                    for t in range(hops(d, h)):
+                        leave(outbox.at[d, t, h, m], ch_s.at[d, t, h, m], ch_r.at[d, t, h, m])
+
+        loop3(chains_sent)
+        for copy in copies:
+            copy.wait()
+
+    across(flows_in[0])
+    multiply(0, 0)
+    chain_send(0, 0, 0)
+    multiply(0, 1)
+    chain_send(0, 0, 1)
+    across(flows_in[1])
+    run(sibling_line, flows_in)
+    gram_partial()
+    multiply(0, 2)
+    chain_send(0, 0, 2)
+    run(finish, flows_in)
     for m in range(3):
-        deltas[m, z] = second[m].reshape(2, half, tokens)
-        spread(0, m)
-
-    def own_to_hbm(m):
-        for h in range(2):
-            to_hbm(m, z, h).start()
-
-    loop3(own_to_hbm)
-
-    for flow in flows_in + flows_gram:
-        sent(flow)
-    for i in range(1, NZ):
-        leave(kpart.at[(z + i) % NZ], kz_s.at[0, i], kz_r.at[0, i])
-        leave(kown.at[z], kz_s.at[1, i], kz_r.at[1, i])
-    for axis, (count, where) in enumerate(spans):
+        multiply(1, m)
+        chain_send(0, 1, m)
+    for m in range(3):
+        chain_send(1, 0, m)
+    gram_reduce()
+    for m in range(3):
+        chain_send(1, 1, m)
+    for m in range(3):
+        chain_send(2, 0, m)
+    gram_rows()
+    run(start, flows_gram)
+    transposed()
+    for m in range(3):
+        chain_send(2, 1, m)
+    for m in range(3):
+        chain_send(3, 0, m)
+    middle(flows_gram[0])
+    middle(flows_gram[1])
+    for m in range(3):
+        chain_send(3, 1, m)
+    for m in range(3):
+        chain_last(m)
+    across(flows_gram[0])
+    across(flows_gram[1])
+    sibling_line(flows_gram[0])
+    finish(flows_gram[0])
+    sibling_line(flows_gram[1])
+    finish(flows_gram[1])
+    gram_whole()
+    energy_own()
+    loop3(functools.partial(spread, 1))
+    energy_wait(0)
+    at_distance(first_pass, 1)
+    energy_wait(1)
+    loop3(functools.partial(spread, 2))
+    early_sent()
+    energy_wait(2)
+    at_distance(second_pass, 0)
+    at_distance(second_pass, 1)
+    at_distance(first_pass, 2)
+    at_distance(second_pass, 2)
+    loop3(functools.partial(spread, 3))
+    at_distance(first_pass, 3)
+    at_distance(second_pass, 3)
+    loop3(functools.partial(spread, 4))
+    at_distance(first_pass, 4)
+    at_distance(second_pass, 4)
+
+    for i, (count, where) in enumerate(spans):
         for q in range(1, count):
-            leave(energy.at[axis], en_s.at[axis, q], en_r.at[axis, q])
-
-    def chains_sent(m):
-        for d in range(2):
-            for h in range(2):
-                for t in range(hops(d, h)):
-                    leave(outbox.at[d, t, h, m], ch_s.at[d, t, h, m], ch_r.at[d, t, h, m])
-
-    loop3(chains_sent)
-    for copy in copies:
-        copy.wait()
-
-    for t in range(1, NZ // 2 + 1):
-        loop3(functools.partial(spread, t))
-
-    def spread_sent(m):
+            leave(energy.at[i], en_s.at[i, q], en_r.at[i, q])
+
+    def late_sent(m):
         for d, sign in enumerate(signs):
             for h in range(2):
                 for t in range(hops(d, h)):
                     leave(
-                        deltas.at[m, (z - sign * t + NZ) % NZ, h],
+                        sums.at[m, (z - sign * t + NZ) % NZ, h],
                         ag_s.at[d, t, m, h], ag_r.at[d, t, m, h],
                     )
         for owner in range(NZ):
-            for h in range(2):
-                to_hbm(m, owner, h).wait()
-
-    loop3(spread_sent)
+            to_hbm(m, owner).wait()
+
+    loop3(late_sent)
 
 
 def gradients(tokens_t, deltas, targets, gate_out, up_out, down_out):
@@ -507,16 +610,19 @@
         vmem((2, hops, 2, 3, 2 * half, tokens // 2), bf16),
         vmem((NZ, block + 8, 128), f32),
         vmem((NZ, block + 8, 128), f32),
-        vmem((NZ, block + 8, 128), f32),
+        vmem((NZ, block, 128), f32),
+        vmem((2, 8, 128), f32),
+        vmem((8, 128), f32),
         vmem((2,) + plane + (span + 1, block, 128), bf16),
         vmem((2, tokens, tokens), bf16),
-        vmem((3, 2 * half, tokens), f32),
-        vmem((3, 2 * half, tokens), f32),
+        vmem((6, 8, tokens), f32),
         vmem((3, NZ, 2, half, tokens), bf16),
+        vmem((3, NZ, 2 * half, tokens), f32),
+        vmem((3, NZ, 2 * half, tokens), bf16),
         vmem((3, 8, 128), f32),
         vmem((3, max(NZ, 2 * NY), 8, 128), f32),
         dma((5,)),
-        dma((3, NZ, 2)),
+        dma((3, NZ)),
         dma((4, 3, max(NX, NY))),
         dma((4, 3, max(NX, NY))),
         dma((2, NZ)),
@@ -532,7 +638,7 @@
     deltas, tokens_t, targets = pl.pallas_call(
         functools.partial(kernel, NZ, NY, NX),
         out_shape=(
-            jax.ShapeDtypeStruct((3, NZ, 2, half, tokens), bf16),
+            jax.ShapeDtypeStruct((3, NZ, 2 * half, tokens), bf16),
             jax.ShapeDtypeStruct((depth, tokens), bf16),
             jax.ShapeDtypeStruct(plane + (block, depth), bf16),
         ),

time: 95.4 us -> 81.6 us (0.86)
  Pallas kernels: 94.1 us -> 80.1 us
    pallas_call x1, Pallas kernels: 88.5 us -> 74.5 us  [shards(): pl.pallas_call(functools.partial(kernel, NZ, NY, NX), out_shape=(jax.Shap...]
where the time goes in v5:
time: 81.6 us; the launch traced here: 80.7 us
  Pallas kernels  80.1 us (98%)
    pallas_call x1, Pallas kernels, shards(): pl.pallas_call(functools.partial(kernel, NZ, NY, NX), out_shape=(jax.Shap...  74.5 us
    pallas_call x1, Pallas kernels, shards(): pl.pallas_call(gradients, grid=(hidden // tile,), out_shape=(jax.ShapeDty...  5.57 us

profile of v5, /device:TPU:2, one launch (start us, length us, event | category | flops | bytes accessed | tf_op | source)
XLA Modules:
  0.0 80.7 jit_solution(14750022689963344970)
XLA Ops:
  0.6 74.5 %shard_map.76 = (bf16[3,8,96,512]{3,2,1,0:T(8,128)(2,1)}, bf16[768,512]{1,0:T(8,128)(2,1)}, bf16[2,4,4,16,768]{4,3,2,1,0:T(8,128)(2,1)}) custom-call(bf16[16,768]{1,0:T(8,128)(2,1)} %features.1, bf16[16,768]{1,0:T(8,128)(2,1)} %cotangent.1, f32[768,768]{1,0:T(8,128)} %gate_master.1, f32[768,768]{1,0:T(8,128)} %up_master.1, f32[768,768]{1,0:T(8,128)} %down_master.1), custom_call_target="tpu_custom_call" | custom-call | flops 1811939328 | bytes 7077888 | tf_op jit(solution)/shard_map/pallas_call | solution.py:638
  75.1 5.6 %shard_map.77 = (bf16[768,768]{1,0:T(8,128)(2,1)}, bf16[768,768]{1,0:T(8,128)(2,1)}, bf16[768,768]{1,0:T(8,128)(2,1)}) custom-call(bf16[768,512]{1,0:T(8,128)(2,1)} %get-tuple-element.6.tokens_t, bf16[3,768,512]{2,1,0:T(8,128)(2,1)} %bitcast.2, bf16[512,768]{1,0:T(8,128)(2,1)} %bitcast.3), custom_call_target="tpu_custom_call" | custom-call | flops 1811939328 | bytes 7471104 | tf_op jit(solution)/shard_map/pallas_call | solution.py:658

commit v6 on v5

--- a/solution.py
+++ b/solution.py
@@ -543,21 +543,29 @@
     finish(flows_gram[1])
     gram_whole()
     energy_own()
-    loop3(functools.partial(spread, 1))
+    spread(1, 0)
     energy_wait(0)
+    spread(1, 1)
+    spread(1, 2)
+    energy_wait(1)
     at_distance(first_pass, 1)
-    energy_wait(1)
-    loop3(functools.partial(spread, 2))
-    early_sent()
+    spread(2, 0)
+    spread(2, 1)
     energy_wait(2)
     at_distance(second_pass, 0)
+    spread(2, 2)
     at_distance(second_pass, 1)
     at_distance(first_pass, 2)
     at_distance(second_pass, 2)
-    loop3(functools.partial(spread, 3))
+    spread(3, 0)
+    spread(3, 1)
+    spread(3, 2)
+    early_sent()
     at_distance(first_pass, 3)
     at_distance(second_pass, 3)
-    loop3(functools.partial(spread, 4))
+    spread(4, 0)
+    spread(4, 1)
+    spread(4, 2)
     at_distance(first_pass, 4)
     at_distance(second_pass, 4)
 

time: 81.6 us -> 80.4 us (0.985)
  Pallas kernels: 80.1 us -> 78.5 us
    pallas_call x1, Pallas kernels: 74.5 us -> 73 us  [shards(): pl.pallas_call(functools.partial(kernel, NZ, NY, NX), out_shape=(jax.Shap...]
where the time goes in v6:
time: 80.4 us; the launch traced here: 79.2 us
  Pallas kernels  78.5 us (98%)
    pallas_call x1, Pallas kernels, shards(): pl.pallas_call(functools.partial(kernel, NZ, NY, NX), out_shape=(jax.Shap...  73 us
    pallas_call x1, Pallas kernels, shards(): pl.pallas_call(gradients, grid=(hidden // tile,), out_shape=(jax.ShapeDty...  5.56 us

profile of v6, /device:TPU:2, one launch (start us, length us, event | category | flops | bytes accessed | tf_op | source)
XLA Modules:
  0.0 79.2 jit_solution(17245888580651387597)
XLA Ops:
  0.6 73.0 %shard_map.76 = (bf16[3,8,96,512]{3,2,1,0:T(8,128)(2,1)}, bf16[768,512]{1,0:T(8,128)(2,1)}, bf16[2,4,4,16,768]{4,3,2,1,0:T(8,128)(2,1)}) custom-call(bf16[16,768]{1,0:T(8,128)(2,1)} %features.1, bf16[16,768]{1,0:T(8,128)(2,1)} %cotangent.1, f32[768,768]{1,0:T(8,128)} %gate_master.1, f32[768,768]{1,0:T(8,128)} %up_master.1, f32[768,768]{1,0:T(8,128)} %down_master.1), custom_call_target="tpu_custom_call" | custom-call | flops 1811939328 | bytes 7077888 | tf_op jit(solution)/shard_map/pallas_call | solution.py:646
  73.6 5.6 %shard_map.77 = (bf16[768,768]{1,0:T(8,128)(2,1)}, bf16[768,768]{1,0:T(8,128)(2,1)}, bf16[768,768]{1,0:T(8,128)(2,1)}) custom-call(bf16[768,512]{1,0:T(8,128)(2,1)} %get-tuple-element.6.tokens_t, bf16[3,768,512]{2,1,0:T(8,128)(2,1)} %bitcast.2, bf16[512,768]{1,0:T(8,128)(2,1)} %bitcast.3), custom_call_target="tpu_custom_call" | custom-call | flops 1811939328 | bytes 7471104 | tf_op jit(solution)/shard_map/pallas_call | solution.py:666
